TPU v7x, 128 devices: a whole 4x4x4 slice. The times are simulated.
128 devices in a mesh: tok: 16 (over y, x_hi, core), hid: 8 (over z, x_lo).
Axes of the slice: x: 4 (x_hi: 2, x_lo: 2; x = x_hi * 2 + x_lo), y: 4, z: 4, core: 2. Of those that a mesh axis runs over, the one named last changes fastest.
Arguments:
- tokens: bfloat16 [24576, 1024], P(('tok', 'hid')), may hold values from -6 to 6
- memory: bfloat16 [49152, 1024], P(('tok', 'hid')), may hold values from -6 to 6
- cotangent: bfloat16 [24576, 1024], P(('tok', 'hid'))
- norm1: bfloat16 [1024], P('tok'), may hold values from 0.25 to 1.75
- w_query: bfloat16 [1024, 1024], P('tok', 'hid'), may hold values from -0.046875 to 0.046875
- w_key: bfloat16 [1024, 512], P('tok', 'hid'), may hold values from -0.1875 to 0.1875
- w_value: bfloat16 [1024, 512], P('tok', 'hid'), may hold values from -0.1875 to 0.1875
- w_out: bfloat16 [1024, 1024], P('hid', 'tok'), may hold values from -0.75 to 0.75
- rel_bias: bfloat16 [32, 16], P('tok', 'hid'), may hold values from -4 to 4
- norm2: bfloat16 [1024], P('tok'), may hold values from 0.25 to 1.75
- cross_query: bfloat16 [1024, 1024], P('tok', 'hid'), may hold values from -0.046875 to 0.046875
- cross_key: bfloat16 [1024, 512], P('tok', 'hid'), may hold values from -0.1875 to 0.1875
- cross_value: bfloat16 [1024, 512], P('tok', 'hid'), may hold values from -0.1875 to 0.1875
- cross_out: bfloat16 [1024, 1024], P('hid', 'tok'), may hold values from -0.75 to 0.75
- norm3: bfloat16 [1024], P('tok'), may hold values from 0.25 to 1.75
- w_gate: bfloat16 [1024, 2816], P('tok', 'hid'), may hold values from -0.1875 to 0.1875
- w_up: bfloat16 [1024, 2816], P('tok', 'hid'), may hold values from -0.1875 to 0.1875
- w_down: bfloat16 [2816, 1024], P('hid', 'tok'), may hold values from -0.109375 to 0.109375
- doc_lengths: int32 [16, 3], P('tok'), may hold values from 1 to 1024, 1536 in all within a row
- memory_slot: int32 [16, 3], P('tok'), may hold values from 0 to 2, each once within a row
- enc_lengths: int32 [16, 3], P('tok'), may hold values from 512 to 1024
- rel_bucket: int32 [1536], replicated, may hold values from 0 to 31
Outputs:
- mixed: bfloat16 [24576, 1024], P(('tok', 'hid'))
- d_tokens: float32 [24576, 1024], P(('tok', 'hid'))
- d_memory: float32 [49152, 1024], P(('tok', 'hid'))
- d_norm1: float32 [1024], P('tok')
- d_w_query: float32 [1024, 1024], P('tok', 'hid')
- d_w_key: float32 [1024, 512], P('tok', 'hid')
- d_w_value: float32 [1024, 512], P('tok', 'hid')
- d_w_out: float32 [1024, 1024], P('hid', 'tok')
- d_rel_bias: float32 [32, 16], P('tok', 'hid')
- d_norm2: float32 [1024], P('tok')
- d_cross_query: float32 [1024, 1024], P('tok', 'hid')
- d_cross_key: float32 [1024, 512], P('tok', 'hid')
- d_cross_value: float32 [1024, 512], P('tok', 'hid')
- d_cross_out: float32 [1024, 1024], P('hid', 'tok')
- d_norm3: float32 [1024], P('tok')
- d_w_gate: float32 [1024, 2816], P('tok', 'hid')
- d_w_up: float32 [1024, 2816], P('tok', 'hid')
- d_w_down: float32 [2816, 1024], P('hid', 'tok')
Inputs may be any that keep to these rules, and one draw needn't show every extreme that they name: `doc_lengths`: each row holds 3 document lengths that sum to 1536; the longest is exactly 1024. `memory_slot`: each row is a permutation of the group's 3 memories.
All inputs are finite; a program needn't handle non-finite values.
Results may differ from a plain program's by a relative error of at most 0.04.
Values may be sent and summed in bfloat16 or wider, within the bound.
A program may use at most 192 MiB of HBM per device.

v0:
```python
import jax
import jax.numpy as jnp
from jax import lax
from jax.experimental import pallas as pl
from jax.experimental.pallas import tpu as pltpu
from jax.sharding import PartitionSpec as P

EPS = 1e-06
HIGH = lax.Precision.HIGHEST
MESH = pl.DeviceIdType.MESH

HDIM = 64
ENC = 1024
FLOAT = jnp.float32
HALF = jnp.bfloat16
TILE = 256
PAIR = 2 * TILE
NEG = -1e30
NT_DIMS = (((1,), (1,)), ((), ()))


def dot(first, second):
    return jnp.dot(first, second, preferred_element_type=FLOAT)


def dot_nt(first, second):
    return lax.dot_general(first, second, NT_DIMS, preferred_element_type=FLOAT)


def stack_heads(block):
    return jnp.concatenate([block[:, :HDIM], block[:, HDIM:]], axis=0)


def unstack_heads(columns):
    return jnp.concatenate(
        [columns[:, :TILE].T, columns[:, TILE:].T], axis=1
    )


def tile_rows(tile):
    return pl.ds(pl.multiple_of(tile * TILE, TILE), TILE)


def lane_positions(first):
    lane = lax.broadcasted_iota(jnp.int32, (1, PAIR), 1)
    return first + jnp.where(lane >= TILE, lane - TILE, lane)


def doc_ends(len_ref):
    first_end = len_ref[0, 0]
    return first_end, first_end + len_ref[0, 1]


def start_of(position, ends):
    return jnp.where(position >= ends[1], ends[1], jnp.where(position >= ends[0], ends[0], 0))


def build_bias(win_ref, bias, tiles):
    for diag in range(tiles):
        for head in range(2):
            row = win_ref[pl.ds(head * 8 + diag, 1), :]
            spread = jnp.broadcast_to(row, (TILE, PAIR))
            rolled = pltpu.roll(spread, 0, 1, stride=1, stride_axis=0)
            bias[diag, :, pl.ds(head * TILE, TILE)] = rolled[:, :TILE]


def online(state, scores, values_t):
    peak, total, acc = state
    new_peak = jnp.maximum(peak, jnp.max(scores, axis=0, keepdims=True))
    shrink = jnp.exp(peak - new_peak)
    weights = jnp.exp(scores - new_peak)
    total = total * shrink + jnp.sum(weights, axis=0, keepdims=True)
    acc = acc * shrink + dot(values_t, weights.astype(HALF))
    return new_peak, total, acc


def fresh_state():
    return (
        jnp.full((1, PAIR), NEG, FLOAT),
        jnp.zeros((1, PAIR), FLOAT),
        jnp.zeros((HDIM, PAIR), FLOAT),
    )


def finish(state, tile, out_ref, lse_ref):
    peak, total, acc = state
    out_ref[tile_rows(tile), :] = unstack_heads(acc / total).astype(HALF)
    lse_ref[pl.ds(tile, 1), :] = peak + jnp.log(total)


def row_prepare(tiles, q_of, do_ref, o_ref, queries, grads, deltas):
    for tile in range(tiles):
        rows = slice(tile * TILE, (tile + 1) * TILE)
        queries[tile] = stack_heads(q_of(rows))
        block = do_ref[rows, :]
        grads[tile] = stack_heads(block)
        product = (block.astype(FLOAT) * o_ref[rows, :].astype(FLOAT)).T
        deltas[tile] = jnp.concatenate(
            [
                jnp.sum(product[:HDIM], axis=0, keepdims=True),
                jnp.sum(product[HDIM:], axis=0, keepdims=True),
            ],
            axis=1,
        )


def fold_diagonals(block):
    half = TILE // 2
    while half >= 8:
        block = block[:half] + pltpu.roll(block[half:], PAIR - half, 1)
        half //= 2
    total = block[0:1]
    for row in range(1, 8):
        total = total + pltpu.roll(block[row : row + 1], PAIR - row, 1)
    return total


def self_backward_kernel(
    len_ref, qkv_ref, win_ref, do_ref, o_ref, lse_ref,
    dqkv_ref, diag_ref,
    keys, values, keys_t, queries, grads, deltas, bias, bias_grad, dq,
):
    tiles = qkv_ref.shape[0] // TILE
    build_bias(win_ref, bias, tiles)
    for tile in range(tiles):
        block = qkv_ref[tile * TILE : (tile + 1) * TILE, 128:256]
        keys[tile] = block[:, :HDIM]
        values[tile] = block[:, HDIM:]
        keys_t[tile] = block[:, :HDIM].astype(FLOAT).T.astype(HALF)
    row_prepare(tiles, lambda rows: qkv_ref[rows, 0:128], do_ref, o_ref, queries, grads, deltas)
    bias_grad[...] = jnp.zeros_like(bias_grad)
    dq[...] = jnp.zeros_like(dq)
    ends = doc_ends(len_ref)
    total_rows = qkv_ref.shape[0]

    @pl.loop(0, tiles)
    def key_tile(other):
        last = other * TILE + TILE - 1
        key_pos = other * TILE + lax.broadcasted_iota(jnp.int32, (TILE, 1), 0)
        stop = jnp.where(last < ends[0], ends[0], jnp.where(last < ends[1], ends[1], total_rows))

        def row_tile(tile, state):
            dk, dv = state
            row_pos = lane_positions(tile * TILE)
            row_start = start_of(row_pos, ends)
            scores = dot_nt(keys[other], queries[tile]) + bias[tile - other]
            allowed = (key_pos <= row_pos) & (key_pos >= row_start)
            scores = jnp.where(allowed, scores, NEG)
            weights = jnp.exp(scores - lse_ref[pl.ds(tile, 1), :])
            d_weights = dot_nt(values[other], grads[tile])
            d_scores = weights * (d_weights - deltas[tile])
            bias_grad[tile - other] += d_scores
            d_half = d_scores.astype(HALF)
            dv = dv + dot(weights.astype(HALF), grads[tile])
            dk = dk + dot(d_half, queries[tile])
            dq[tile] += dot(keys_t[other], d_half)
            return dk, dv

        zero = jnp.zeros((TILE, HDIM), FLOAT)
        dk, dv = lax.fori_loop(other, (stop - 1) // TILE + 1, row_tile, (zero, zero))
        dqkv_ref[tile_rows(other), 128:256] = jnp.concatenate([dk, dv], axis=1).astype(HALF)

    for tile in range(tiles):
        dqkv_ref[tile * TILE : (tile + 1) * TILE, 0:128] = unstack_heads(dq[tile]).astype(HALF)
        for head in range(2):
            part = bias_grad[tile, :, head * TILE : (head + 1) * TILE]
            part = jnp.concatenate([part, jnp.zeros_like(part)], axis=1)
            diag_ref[pl.ds(tile * 2 + head, 1), :] = fold_diagonals(part)


def self_backward(doc_lens, qkv, windows, d_out, out, lse):
    rows = qkv.shape[0]
    tiles = rows // TILE
    vmem = pl.BlockSpec(memory_space=pltpu.VMEM)
    return pl.pallas_call(
        self_backward_kernel,
        out_shape=(
            jax.ShapeDtypeStruct((rows, 256), HALF),
            jax.ShapeDtypeStruct((2 * tiles, PAIR), FLOAT),
        ),
        in_specs=[pl.BlockSpec(memory_space=pltpu.SMEM)] + [vmem] * 5,
        out_specs=(vmem, vmem),
        scratch_shapes=[
            pltpu.VMEM((tiles, TILE, HDIM), HALF),
            pltpu.VMEM((tiles, TILE, HDIM), HALF),
            pltpu.VMEM((tiles, HDIM, TILE), HALF),
            pltpu.VMEM((tiles, PAIR, HDIM), HALF),
            pltpu.VMEM((tiles, PAIR, HDIM), HALF),
            pltpu.VMEM((tiles, 1, PAIR), FLOAT),
            pltpu.VMEM((tiles, TILE, PAIR), FLOAT),
            pltpu.VMEM((tiles, TILE, PAIR), FLOAT),
            pltpu.VMEM((tiles, HDIM, PAIR), FLOAT),
        ],
        compiler_params=pltpu.CompilerParams(vmem_limit_bytes=48 * 2**20),
    )(doc_lens, qkv, windows, d_out, out, lse)


def cross_forward_kernel(
    len_ref, slot_ref, enc_ref, q_ref, kv_ref, out_ref, lse_ref, keys, values_t
):
    tiles = q_ref.shape[0] // TILE
    key_tiles = kv_ref.shape[0] // TILE
    for tile in range(key_tiles):
        block = kv_ref[tile * TILE : (tile + 1) * TILE, :]
        keys[tile] = block[:, :HDIM]
        values_t[tile] = block[:, HDIM:].astype(FLOAT).T.astype(HALF)
    ends = doc_ends(len_ref)

    def doc_at(position):
        return (position >= ends[0]).astype(jnp.int32) + (position >= ends[1]).astype(jnp.int32)

    @pl.loop(0, tiles)
    def row_tile(tile):
        first = tile * TILE
        queries = stack_heads(q_ref[tile_rows(tile), :])
        row_doc = doc_at(lane_positions(first))

        def one_doc(doc, state):
            slot = slot_ref[0, doc]
            valid = enc_ref[0, slot]
            mine = row_doc == doc
            base = slot * (ENC // TILE)

            def key_tile(other, inner):
                scores = dot_nt(keys[base + other], queries)
                key_pos = other * TILE + lax.broadcasted_iota(jnp.int32, (TILE, 1), 0)
                scores = jnp.where(mine & (key_pos < valid), scores, NEG)
                return online(inner, scores, values_t[base + other])

            return lax.fori_loop(0, (valid + TILE - 1) // TILE, key_tile, state)

        state = lax.fori_loop(doc_at(first), doc_at(first + TILE - 1) + 1, one_doc, fresh_state())
        finish(state, tile, out_ref, lse_ref)


def cross_forward(doc_lens, slots, enc_lens, queries, kv):
    rows = queries.shape[0]
    key_tiles = kv.shape[0] // TILE
    vmem = pl.BlockSpec(memory_space=pltpu.VMEM)
    return pl.pallas_call(
        cross_forward_kernel,
        out_shape=(
            jax.ShapeDtypeStruct((rows, 128), HALF),
            jax.ShapeDtypeStruct((8, PAIR), FLOAT),
        ),
        in_specs=[pl.BlockSpec(memory_space=pltpu.SMEM)] * 3 + [vmem] * 2,
        out_specs=(vmem, vmem),
        scratch_shapes=[
            pltpu.VMEM((key_tiles, TILE, HDIM), HALF),
            pltpu.VMEM((key_tiles, HDIM, TILE), HALF),
        ],
        compiler_params=pltpu.CompilerParams(vmem_limit_bytes=48 * 2**20),
    )(doc_lens, slots, enc_lens, queries, kv)


def cross_backward_kernel(
    len_ref, slot_ref, enc_ref, q_ref, kv_ref, do_ref, o_ref, lse_ref,
    dq_ref, dkv_ref,
    keys, values, keys_t, queries, grads, deltas, dq,
):
    tiles = q_ref.shape[0] // TILE
    key_tiles = kv_ref.shape[0] // TILE
    for tile in range(key_tiles):
        block = kv_ref[tile * TILE : (tile + 1) * TILE, :]
        keys[tile] = block[:, :HDIM]
        values[tile] = block[:, HDIM:]
        keys_t[tile] = block[:, :HDIM].astype(FLOAT).T.astype(HALF)
    row_prepare(tiles, lambda rows: q_ref[rows, :], do_ref, o_ref, queries, grads, deltas)
    dq[...] = jnp.zeros_like(dq)
    dkv_ref[...] = jnp.zeros_like(dkv_ref)
    ends = doc_ends(len_ref)
    total_rows = q_ref.shape[0]

    @pl.loop(0, 3)
    def one_doc(doc):
        start = jnp.where(doc == 0, 0, jnp.where(doc == 1, ends[0], ends[1]))
        stop = jnp.where(doc == 0, ends[0], jnp.where(doc == 1, ends[1], total_rows))
        slot = slot_ref[0, doc]
        valid = enc_ref[0, slot]
        base = slot * (ENC // TILE)

        @pl.loop(0, (valid + TILE - 1) // TILE)
        def key_tile(other):
            key_pos = other * TILE + lax.broadcasted_iota(jnp.int32, (TILE, 1), 0)
            place = base + other

            def row_tile(tile, state):
                dk, dv = state
                row_pos = lane_positions(tile * TILE)
                scores = dot_nt(keys[place], queries[tile])
                allowed = (row_pos >= start) & (row_pos < stop) & (key_pos < valid)
                scores = jnp.where(allowed, scores, NEG)
                weights = jnp.exp(scores - lse_ref[pl.ds(tile, 1), :])
                d_weights = dot_nt(values[place], grads[tile])
                d_half = (weights * (d_weights - deltas[tile])).astype(HALF)
                dv = dv + dot(weights.astype(HALF), grads[tile])
                dk = dk + dot(d_half, queries[tile])
                dq[tile] += dot(keys_t[place], d_half)
                return dk, dv

            zero = jnp.zeros((TILE, HDIM), FLOAT)
            dk, dv = lax.fori_loop(
                start // TILE, (stop - 1) // TILE + 1, row_tile, (zero, zero)
            )
            dkv_ref[tile_rows(place), :] = jnp.concatenate([dk, dv], axis=1).astype(HALF)

    for tile in range(tiles):
        dq_ref[tile * TILE : (tile + 1) * TILE, :] = unstack_heads(dq[tile]).astype(HALF)


def cross_backward(doc_lens, slots, enc_lens, queries, kv, d_out, out, lse):
    rows = queries.shape[0]
    tiles = rows // TILE
    key_tiles = kv.shape[0] // TILE
    vmem = pl.BlockSpec(memory_space=pltpu.VMEM)
    return pl.pallas_call(
        cross_backward_kernel,
        out_shape=(
            jax.ShapeDtypeStruct((rows, 128), HALF),
            jax.ShapeDtypeStruct((kv.shape[0], 128), HALF),
        ),
        in_specs=[pl.BlockSpec(memory_space=pltpu.SMEM)] * 3 + [vmem] * 5,
        out_specs=(vmem, vmem),
        scratch_shapes=[
            pltpu.VMEM((key_tiles, TILE, HDIM), HALF),
            pltpu.VMEM((key_tiles, TILE, HDIM), HALF),
            pltpu.VMEM((key_tiles, HDIM, TILE), HALF),
            pltpu.VMEM((tiles, PAIR, HDIM), HALF),
            pltpu.VMEM((tiles, PAIR, HDIM), HALF),
            pltpu.VMEM((tiles, 1, PAIR), FLOAT),
            pltpu.VMEM((tiles, HDIM, PAIR), FLOAT),
        ],
        compiler_params=pltpu.CompilerParams(vmem_limit_bytes=48 * 2**20),
    )(doc_lens, slots, enc_lens, queries, kv, d_out, out, lse)


WIDTH = 1920
SHARD = 64
FF_PAD = 384
PAD_AT = 1536 + 352
CUTS = ((0, 640), (640, 640), (1280, 640))
ORDERS = ("zyx", "yxz", "xzy")


class Torus:
    def __init__(self):
        tok, hid = lax.axis_index("tok"), lax.axis_index("hid")
        self.core = lax.rem(tok, 2)
        self.pos = {
            "x": lax.rem(tok // 2, 2) * 2 + lax.rem(hid, 2),
            "y": tok // 4,
            "z": hid // 2,
        }

    def moved(self, axis, step):
        place = dict(self.pos)
        place[axis] = lax.rem(place[axis] + step + 4, 4)
        return place

    def device(self, place, core=None):
        core = self.core if core is None else core
        return (
            (place["y"] * 2 + place["x"] // 2) * 2 + core,
            place["z"] * 2 + lax.rem(place["x"], 2),
        )

    def neighbour(self, axis, step):
        return self.device(self.moved(axis, step))

    def sibling(self):
        return self.device(self.pos, 1 - self.core)

    def greet(self):
        barrier = pltpu.get_barrier_semaphore()
        peers = [self.neighbour(axis, step) for axis in "xyz" for step in (1, -1)]
        for peer in peers + [self.sibling()]:
            pl.semaphore_signal(barrier, inc=1, device_id=peer, device_id_type=MESH)
        return barrier


def block_index(place, whole):
    return (
        slice(None) if "z" in whole else place["z"],
        slice(None) if "x" in whole else lax.rem(place["x"], 2),
        slice(None) if "y" in whole else place["y"],
        slice(None) if "x" in whole else place["x"] // 2,
    )


def whole_dims(whole):
    dims = (4,) if "z" in whole else ()
    dims += (2,) if "x" in whole else ()
    dims += (4,) if "y" in whole else ()
    return dims + ((2,) if "x" in whole else ())


class Flow:
    def __init__(self, torus, out_ref, cuts, orders, sems):
        self.torus, self.out_ref, self.cuts, self.orders = torus, out_ref, cuts, orders
        self.sems = sems
        self.rows = out_ref.shape[5]
        self.sends, self.siblings = [], []
        self.last = {}

    def view(self, place, whole, cut, rows=None):
        rows = (0, self.rows) if rows is None else rows
        return self.out_ref.at[
            block_index(place, whole) + (self.torus.core, pl.ds(*rows), pl.ds(*cut))
        ]

    def copy(self, ref, target, first, log):
        at = len(log)
        copy = pltpu.make_async_remote_copy(
            src_ref=ref, dst_ref=ref,
            send_sem=self.sems[first].at[at], recv_sem=self.sems[first + 1].at[at],
            device_id=target, device_id_type=MESH,
        )
        copy.start()
        log.append(copy)
        return copy

    def to_sibling(self, place, whole, cut):
        self.copy(self.view(place, whole, cut), self.torus.sibling(), 2, self.siblings)

    def plan(self, stage):
        for part, cut in enumerate(self.cuts):
            yield part, cut, self.orders[part][stage], self.orders[part][:stage]

    def near(self, stage):
        torus = self.torus
        for part, cut, axis, whole in self.plan(stage):
            if stage == 0:
                self.to_sibling(torus.pos, "", cut)
            ref = self.view(torus.pos, whole, cut)
            self.last[part] = [
                self.copy(ref, torus.neighbour(axis, step), 0, self.sends) for step in (1, -1)
            ]

    def far(self, stage):
        torus, half = self.torus, self.rows // 2
        for part, cut, axis, whole in self.plan(stage):
            copies = []
            for copy, step, first in zip(self.last[part], (1, -1), (0, half)):
                origin = torus.moved(axis, -step)
                copy.wait_recv()
                if half >= 16:
                    ref = self.view(origin, whole, cut, (first, half))
                    copies.append(self.copy(ref, torus.neighbour(axis, step), 0, self.sends))
                elif step == 1:
                    ref = self.view(origin, whole, cut)
                    copies.append(self.copy(ref, torus.neighbour(axis, step), 0, self.sends))
                self.to_sibling(origin, whole, cut)
            self.last[part] = copies

    def done(self, stage):
        for part, cut, axis, whole in self.plan(stage):
            for copy in self.last[part]:
                copy.wait_recv()
            self.to_sibling(self.torus.moved(axis, 2), whole, cut)

    def arrived(self):
        for copy in self.siblings:
            copy.wait_recv()

    def finish(self):
        for copy in self.sends + self.siblings:
            copy.wait_send()


def flow_sems(parts, split):
    sends = parts * 3 * (2 + split)
    return [pltpu.SemaphoreType.DMA((sends,))] * 2 + [pltpu.SemaphoreType.DMA((parts * 10,))] * 2


class Trade:
    def __init__(self, src, land, sems):
        self.src, self.land, self.sems = src, land, sems
        self.me = lax.axis_index("hid")
        self.tok = lax.axis_index("tok")

    def copy(self, step):
        target = lax.rem(self.me + step, 8)
        return pltpu.make_async_remote_copy(
            src_ref=self.src(target), dst_ref=self.land(self.me),
            send_sem=self.sems[0].at[step - 1], recv_sem=self.sems[1].at[step - 1],
            device_id=(self.tok, target), device_id_type=MESH,
        )

    def start(self, step):
        self.copy(step).start()

    def start_all(self):
        for step in range(1, 8):
            self.start(step)

    def arrived(self):
        for step in range(1, 8):
            self.copy(step).wait_recv()

    def finish(self):
        for step in range(1, 8):
            self.copy(step).wait_send()


def trade_sems():
    return [pltpu.SemaphoreType.DMA((7,))] * 2


def greet_all(torus):
    barrier = pltpu.get_barrier_semaphore()
    tok, me = lax.axis_index("tok"), lax.axis_index("hid")
    outside = 2 * lax.rem(me, 2) - 1
    peers = [(tok, lax.rem(me + step, 8)) for step in range(1, 8)]
    peers += [torus.neighbour("y", 1), torus.neighbour("y", -1), torus.neighbour("x", outside)]
    peers += [torus.sibling()]
    for peer in peers:
        pl.semaphore_signal(barrier, inc=1, device_id=peer, device_id_type=MESH)
    return barrier, len(peers)


def greet_hid():
    barrier = pltpu.get_barrier_semaphore()
    tok, me = lax.axis_index("tok"), lax.axis_index("hid")
    for step in range(1, 8):
        pl.semaphore_signal(
            barrier, inc=1, device_id=(tok, lax.rem(me + step, 8)), device_id_type=MESH
        )
    return barrier


def rows_at(index, rows):
    return pl.ds(pl.multiple_of(index * rows, 64), rows)


def each_target(body):
    me = lax.axis_index("hid")

    @pl.loop(1, 9)
    def one(step):
        body(step, lax.rem(me + step, 8), step < 8)


def scale_of(row_vals):
    return lax.rsqrt(jnp.mean(row_vals * row_vals, axis=-1, keepdims=True) + EPS)


def norm_backward(row_vals, gain, gradient):
    scale = scale_of(row_vals)
    normal = row_vals * scale
    d_gain = jnp.sum(gradient * normal, axis=0, keepdims=True)
    weighted = gradient * gain
    inner = jnp.mean(weighted * normal, axis=-1, keepdims=True)
    return scale * (weighted - normal * inner), d_gain


def forward_kernel(
    packed_ref, small_ref, tok_ref, mem_ref, len_ref, bucket_ref,
    wf_ref, wa_ref, gain_ref, win_ref, h1_ref, h2_ref, qkv_ref, kv_ref,
    o1_ref, o1r_ref, lse_ref, x1_ref, q2_ref,
    wa, small, send_qkv, send_kv, send_q2, keys, values_t, bias, own_sem, *sems,
):
    torus = Torus()
    me = lax.axis_index("hid")
    rows, mem_rows = tok_ref.shape[0], mem_ref.shape[0]
    tiles = qkv_ref.shape[0] // TILE
    barrier, count = greet_all(torus)
    here = block_index(torus.pos, "") + (torus.core,)
    owns = [
        pltpu.make_async_copy(packed_ref.at[:, pl.ds(0, 768)], wa.at[here], own_sem.at[0]),
        pltpu.make_async_copy(packed_ref.at[:, pl.ds(768, 1152)], wf_ref.at[here], own_sem.at[1]),
        pltpu.make_async_copy(small_ref, small.at[here], own_sem.at[2]),
    ]
    for own in owns:
        own.start()
    for own in owns:
        own.wait()
    pl.semaphore_wait(barrier, count)

    cuts_a = tuple((at, 256) for at in (0, 256, 512))
    cuts_f = tuple((at, 384) for at in (0, 384, 768))
    flow_a = Flow(torus, wa, cuts_a, ORDERS, sems[0:4])
    flow_f = Flow(torus, wf_ref, cuts_f, ORDERS, sems[4:8])
    flow_s = Flow(torus, small, ((0, 128),), ORDERS, sems[8:12])
    flow_a.near(0)
    flow_s.near(0)
    flow_f.near(0)
    flow_a.far(0)
    flow_s.far(0)
    flow_f.far(0)
    for stage in (1, 2):
        flow_a.done(stage - 1)
        flow_s.done(stage - 1)
        flow_a.near(stage)
        flow_s.near(stage)
        if stage == 1:
            flow_f.done(0)
            flow_f.near(1)
        flow_a.far(stage)
        flow_s.far(stage)
        if stage == 1:
            flow_f.far(1)
    flow_s.done(2)
    flow_f.done(1)
    flow_s.arrived()
    z, xlo = torus.pos["z"], lax.rem(me, 2)
    gain_parts = []
    heads = [jnp.zeros((8, PAIR), FLOAT), jnp.zeros((8, PAIR), FLOAT)]
    buckets = bucket_ref[...]
    for pair in range(8):
        blocks = [small[z, xlo, pair // 2, pair % 2, core].astype(FLOAT) for core in range(2)]
        gain_parts.append((blocks[0] + blocks[1])[0:8])
        for core in range(2):
            for part in range(2):
                bucket = (pair * 2 + core) * 2 + part
                for head in range(2):
                    at = 3 + part * 2 + head
                    value = blocks[core][at : at + 1]
                    value = jnp.concatenate([value] * 4, axis=1)
                    heads[head] = jnp.where(buckets == bucket, value, heads[head])
    gain_ref[...] = jnp.concatenate(gain_parts, axis=1)
    win_ref[0:8] = heads[0]
    win_ref[8:16] = heads[1]
    residual = tok_ref[...].astype(FLOAT)
    h1_ref[...] = (residual * scale_of(residual) * gain_ref[0:1, :]).astype(HALF)
    build_bias(win_ref, bias, tiles)

    flow_a.done(2)
    flow_f.near(2)
    flow_a.arrived()
    keep = pltpu.make_async_copy(wa, wa_ref, own_sem.at[0])
    keep.start()

    def weights(j, first, width):
        block = wa[j // 2, lax.rem(j, 2), :, :, :, :, first : first + width]
        return block.reshape(16 * SHARD, width)

    qkv_trade = Trade(
        lambda j: send_qkv.at[j], lambda j: qkv_ref.at[rows_at(j, rows)], sems[12:14]
    )
    kv_trade = Trade(
        lambda j: send_kv.at[j], lambda j: kv_ref.at[rows_at(j, mem_rows)], sems[14:16]
    )
    o1_trade = Trade(
        lambda j: o1_ref.at[rows_at(j, rows)], lambda j: o1r_ref.at[j], sems[16:18]
    )
    q2_trade = Trade(
        lambda j: send_q2.at[j], lambda j: q2_ref.at[rows_at(j, rows)], sems[18:20]
    )

    def spread(trade, left_ref, first, width, send_ref, land_ref):
        def one(step, j, remote):
            value = dot(left_ref[...], weights(j, first, width)).astype(HALF)

            @pl.when(remote)
            def _():
                send_ref[j] = value
                trade.start(step)

            @pl.when(jnp.logical_not(remote))
            def _():
                land_ref[rows_at(me, left_ref.shape[0]), :] = value

        each_target(one)

    spread(qkv_trade, h1_ref, 0, 256, send_qkv, qkv_ref)
    spread(kv_trade, mem_ref, 512, 128, send_kv, kv_ref)
    qkv_trade.arrived()
    flow_f.far(2)

    for tile in range(tiles):
        block = qkv_ref[tile * TILE : (tile + 1) * TILE, 128:256]
        keys[tile] = block[:, :HDIM]
        values_t[tile] = block[:, HDIM:].astype(FLOAT).T.astype(HALF)
    ends = doc_ends(len_ref)

    @pl.loop(0, tiles)
    def row_tile(tile):
        queries = stack_heads(qkv_ref[tile_rows(tile), 0:128])
        row_pos = lane_positions(tile * TILE)
        row_start = start_of(row_pos, ends)

        def key_tile(other, state):
            scores = dot_nt(keys[other], queries) + bias[tile - other]
            key_pos = other * TILE + lax.broadcasted_iota(jnp.int32, (TILE, 1), 0)
            allowed = (key_pos <= row_pos) & (key_pos >= row_start)
            scores = jnp.where(allowed, scores, NEG)
            return online(state, scores, values_t[other])

        finish(lax.fori_loop(0, tile + 1, key_tile, fresh_state()), tile, o1_ref, lse_ref)

    o1_trade.start_all()
    o1r_ref[me] = o1_ref[rows_at(me, rows), :]
    o1_trade.arrived()
    total = tok_ref[...].astype(FLOAT)
    for pair in range(4):
        left = jnp.concatenate([o1r_ref[2 * pair], o1r_ref[2 * pair + 1]], axis=1)
        right = jnp.concatenate(
            [weights(2 * pair, 256, 128), weights(2 * pair + 1, 256, 128)], axis=1
        )
        total = total + dot_nt(left, right)
    x1_ref[...] = total
    h2_ref[...] = (total * scale_of(total) * gain_ref[1:2, :]).astype(HALF)
    spread(q2_trade, h2_ref, 384, 128, send_q2, q2_ref)
    flow_f.done(2)
    q2_trade.arrived()
    kv_trade.arrived()
    flow_f.arrived()
    for trade in (qkv_trade, kv_trade, o1_trade, q2_trade):
        trade.finish()
    for flow in (flow_a, flow_f, flow_s):
        flow.finish()
    keep.wait()


def forward(packed, small, tokens, memory, doc_lens, buckets):
    rows, mem_rows = tokens.shape[0], memory.shape[0]
    group, keys = rows * 8, mem_rows * 8
    tiles = group // TILE
    vmem = pl.BlockSpec(memory_space=pltpu.VMEM)
    anywhere = pl.BlockSpec(memory_space=pl.ANY)
    shape = jax.ShapeDtypeStruct
    places = (4, 2, 4, 2, 2)
    return pl.pallas_call(
        forward_kernel,
        out_shape=(
            shape(places + (SHARD, 1152), HALF),
            shape(places + (SHARD, 768), HALF),
            shape((8, 1024), FLOAT),
            shape((16, PAIR), FLOAT),
            shape((rows, 1024), HALF),
            shape((rows, 1024), HALF),
            shape((group, 256), HALF),
            shape((keys, 128), HALF),
            shape((group, 128), HALF),
            shape((8, rows, 128), HALF),
            shape((8, PAIR), FLOAT),
            shape((rows, 1024), FLOAT),
            shape((group, 128), HALF),
        ),
        in_specs=[anywhere, anywhere, vmem, vmem, pl.BlockSpec(memory_space=pltpu.SMEM), vmem],
        out_specs=(anywhere, anywhere) + (vmem,) * 11,
        scratch_shapes=[
            pltpu.VMEM(places + (SHARD, 768), HALF),
            pltpu.VMEM(places + (16, 128), HALF),
            pltpu.VMEM((8, rows, 256), HALF),
            pltpu.VMEM((8, mem_rows, 128), HALF),
            pltpu.VMEM((8, rows, 128), HALF),
            pltpu.VMEM((tiles, TILE, HDIM), HALF),
            pltpu.VMEM((tiles, HDIM, TILE), HALF),
            pltpu.VMEM((tiles, TILE, PAIR), FLOAT),
            pltpu.SemaphoreType.DMA((3,)),
        ]
        + flow_sems(3, 2) + flow_sems(3, 2) + flow_sems(1, 1)
        + trade_sems() * 4,
        compiler_params=pltpu.CompilerParams(
            collective_id=0, has_side_effects=True, vmem_limit_bytes=56 * 2**20
        ),
    )(packed, small, tokens, memory, doc_lens, buckets)


def middle_kernel(
    o2_ref, x1_ref, cot_ref, gain_ref, wa_ref, wf_ref,
    o2r_ref, mixed_ref, h3_ref, hid_ref, dgu_ref, g2_ref, do_ref, dnorm_ref,
    w_out, w_ff, send_do, out_acc, in_acc, load_sem, ff_sem, *sems,
):
    me = lax.axis_index("hid")
    rows = x1_ref.shape[0]
    barrier = greet_hid()
    load = pltpu.make_async_copy(wa_ref.at[:, :, pl.ds(640, 128)], w_out, load_sem)
    load.start()

    def fetch(j):
        slot = lax.rem(j, 2)
        return pltpu.make_async_copy(wf_ref.at[j], w_ff.at[slot], ff_sem.at[slot])

    fetch(0).start()
    o2_trade = Trade(
        lambda j: o2_ref.at[rows_at(j, rows)], lambda j: o2r_ref.at[j], sems[0:2]
    )
    do_trade = Trade(
        lambda j: send_do.at[j], lambda j: do_ref.at[rows_at(j, rows)], sems[2:4]
    )
    o2r_ref[me] = o2_ref[rows_at(me, rows), :]
    pl.semaphore_wait(barrier, 7)
    o2_trade.start_all()
    load.wait()
    o2_trade.arrived()
    x_two = x1_ref[...]
    for pair in range(4):
        left = jnp.concatenate([o2r_ref[2 * pair], o2r_ref[2 * pair + 1]], axis=1)
        right = jnp.concatenate([w_out[2 * pair], w_out[2 * pair + 1]], axis=1)
        x_two = x_two + dot_nt(left, right)
    out_acc[...] = x_two
    g2_ref[...] = x_two
    in_acc[...] = jnp.zeros_like(in_acc)
    h3_ref[...] = (x_two * scale_of(x_two) * gain_ref[2:3, :]).astype(HALF)

    @pl.loop(0, 8)
    def one_block(j):
        @pl.when(j < 7)
        def _():
            fetch(j + 1).start()

        fetch(j).wait()
        slot = lax.rem(j, 2)
        gate_up = dot(h3_ref[...], w_ff[slot, :, 0:768])
        gate, up = gate_up[:, :FF_PAD], gate_up[:, FF_PAD:]
        d_hidden = dot(cot_ref[...], w_ff[slot, :, 768:1152])
        curve = 0.7978845608028654 * (gate + 0.044715 * gate * gate * gate)
        bend = jnp.tanh(curve)
        gelu = 0.5 * gate * (1.0 + bend)
        slope = 0.5 * (1.0 + bend) + 0.5 * gate * (1.0 - bend * bend) * (
            0.7978845608028654 * (1.0 + 3.0 * 0.044715 * gate * gate)
        )
        hidden = (gelu * up).astype(HALF)
        hid_ref[j] = hidden
        d_both = jnp.concatenate([d_hidden * up * slope, d_hidden * gelu], axis=1).astype(HALF)
        dgu_ref[j] = d_both
        out_acc[...] += dot_nt(hidden, w_ff[slot, :, 768:1152])
        in_acc[...] += dot_nt(d_both, w_ff[slot, :, 0:768])

    mixed_ref[...] = out_acc[...].astype(HALF)
    d_inner, d_gain = norm_backward(g2_ref[...], gain_ref[2:3, :], in_acc[...])
    dnorm_ref[...] = d_gain
    g_two = cot_ref[...].astype(FLOAT) + d_inner
    g2_ref[...] = g_two
    in_acc[...] = g_two

    def one(step, j, remote):
        value = dot(in_acc[...].astype(HALF), w_out[j]).astype(HALF)

        @pl.when(remote)
        def _():
            send_do[j] = value
            do_trade.start(step)

        @pl.when(jnp.logical_not(remote))
        def _():
            do_ref[rows_at(me, rows), :] = value

    each_target(one)
    do_trade.arrived()
    o2_trade.finish()
    do_trade.finish()


def middle(o_two, x_one, cotangent, gains, wa, wf):
    rows = x_one.shape[0]
    vmem = pl.BlockSpec(memory_space=pltpu.VMEM)
    anywhere = pl.BlockSpec(memory_space=pl.ANY)
    shape = jax.ShapeDtypeStruct
    return pl.pallas_call(
        middle_kernel,
        out_shape=(
            shape((8, rows, 128), HALF),
            shape((rows, 1024), HALF),
            shape((rows, 1024), HALF),
            shape((8, rows, FF_PAD), HALF),
            shape((8, rows, 2 * FF_PAD), HALF),
            shape((rows, 1024), FLOAT),
            shape((rows * 8, 128), HALF),
            shape((1, 1024), FLOAT),
        ),
        in_specs=[vmem] * 4 + [anywhere] * 2,
        out_specs=(vmem,) * 8,
        scratch_shapes=[
            pltpu.VMEM((8, 1024, 128), HALF),
            pltpu.VMEM((2, 1024, 1152), HALF),
            pltpu.VMEM((8, rows, 128), HALF),
            pltpu.VMEM((rows, 1024), FLOAT),
            pltpu.VMEM((rows, 1024), FLOAT),
            pltpu.SemaphoreType.DMA,
            pltpu.SemaphoreType.DMA((2,)),
        ]
        + trade_sems() * 2,
        compiler_params=pltpu.CompilerParams(
            collective_id=2, has_side_effects=True, vmem_limit_bytes=56 * 2**20
        ),
    )(o_two, x_one, cotangent, gains, wa, wf)


def scatter_kernel(
    g_ref, out_ref, acc, core_in, *rest
):
    buffers = rest[:18]
    core_send, core_recv, load_sem, send_sem, recv_sem = rest[18:]
    torus = Torus()
    barrier = torus.greet()
    pl.semaphore_wait(barrier, 7)

    def add_blocks(place, whole, rows, cut, sources):
        dims = whole_dims(whole)
        count = 1
        for dim in dims:
            count *= dim

        def one(step):
            index, rest_of = [], step
            for dim in reversed(dims):
                index.append(lax.rem(rest_of, dim))
                rest_of = rest_of // dim
            index = index[::-1]
            left = iter(index)
            at = tuple(
                next(left) if isinstance(entry, slice) else entry
                for entry in block_index(place, whole)
            )
            where = at + (pl.ds(*rows), pl.ds(*cut))
            total = acc[where].astype(FLOAT)
            for source in sources:
                total = total + source(at, tuple(index)).astype(FLOAT)
            acc[where] = total.astype(acc.dtype)

        if count == 1:
            one(jnp.int32(0))
        else:
            pl.loop(0, count)(one)

    core_copies = {}
    for step in (2, 1, -1, 0):
        for part, cut in enumerate(CUTS):
            axis, whole = ORDERS[part][2], ORDERS[part][:2]
            at = block_index(torus.moved(axis, step), whole)
            cols = (slice(None), pl.ds(*cut))
            number = len(core_copies)
            remote = pltpu.make_async_remote_copy(
                src_ref=g_ref.at[at + (1 - torus.core,) + cols],
                dst_ref=core_in.at[at + cols],
                send_sem=core_send.at[number],
                recv_sem=core_recv.at[number],
                device_id=torus.sibling(),
                device_id_type=MESH,
            )
            remote.start()
            here = pltpu.make_async_copy(
                g_ref.at[at + (torus.core,) + cols], acc.at[at + cols], load_sem.at[number]
            )
            here.start()
            core_copies[step, part] = (remote, here)

    def core_sum(step, part):
        remote, here = core_copies[step, part]
        remote.wait_recv()
        here.wait()
        axis, whole, cut = ORDERS[part][2], ORDERS[part][:2], CUTS[part]
        add_blocks(
            torus.moved(axis, step), whole, (0, SHARD), cut,
            [lambda at, index: core_in[at + (slice(None), pl.ds(*cut))]],
        )

    sends = []

    def send(src, dst, target):
        at = len(sends)
        copy = pltpu.make_async_remote_copy(
            src_ref=src, dst_ref=dst, send_sem=send_sem.at[at], recv_sem=recv_sem.at[at],
            device_id=target, device_id_type=MESH,
        )
        copy.start()
        sends.append(copy)
        return copy

    def view(place, whole, rows, cut):
        return acc.at[block_index(place, whole) + (pl.ds(*rows), pl.ds(*cut))]

    def landed(buffer, slot):
        return lambda at, index: buffer[(slot,) + index]

    for stage in (2, 1, 0):
        far, near = [], []
        for part, cut in enumerate(CUTS):
            if stage == 2:
                core_sum(2, part)
            axis, whole = ORDERS[part][stage], ORDERS[part][:stage]
            buffer = buffers[(stage * 3 + part) * 2]
            across = torus.moved(axis, 2)
            far.append((
                send(view(across, whole, (0, 32), cut), buffer.at[0], torus.neighbour(axis, 1)),
                send(view(across, whole, (32, 32), cut), buffer.at[1], torus.neighbour(axis, -1)),
            ))
        for part, cut in enumerate(CUTS):
            if stage == 2:
                core_sum(1, part)
                core_sum(-1, part)
            axis, whole = ORDERS[part][stage], ORDERS[part][:stage]
            got, last = buffers[(stage * 3 + part) * 2 : (stage * 3 + part) * 2 + 2]
            pair = []
            for slot, step, rows in ((0, 1, (0, 32)), (1, -1, (32, 32))):
                place = torus.moved(axis, step)
                far[part][slot].wait_recv()
                add_blocks(place, whole, rows, cut, [landed(got, slot)])
                pair.append(
                    send(view(place, whole, (0, SHARD), cut), last.at[slot], torus.neighbour(axis, step))
                )
            near.append(pair)
        for part, cut in enumerate(CUTS):
            if stage == 2:
                core_sum(0, part)
            whole = ORDERS[part][:stage]
            last = buffers[(stage * 3 + part) * 2 + 1]
            near[part][0].wait_recv()
            near[part][1].wait_recv()
            if stage > 0:
                add_blocks(torus.pos, whole, (0, SHARD), cut, [landed(last, 0), landed(last, 1)])
            else:
                mine = acc[block_index(torus.pos, "") + (slice(None), pl.ds(*cut))]
                out_ref[:, pl.ds(*cut)] = (
                    mine.astype(FLOAT) + last[0].astype(FLOAT) + last[1].astype(FLOAT)
                )
    for copy in sends:
        copy.wait_send()
    for remote, _ in core_copies.values():
        remote.wait_send()


def scatter_grads(grads):
    scratch = [pltpu.VMEM((4, 2, 4, 2, SHARD, WIDTH), HALF)] * 2
    for stage in range(3):
        for part, cut in enumerate(CUTS):
            dims = whole_dims(ORDERS[part][:stage])
            scratch.append(pltpu.VMEM((2,) + dims + (32, cut[1]), HALF))
            scratch.append(pltpu.VMEM((2,) + dims + (SHARD, cut[1]), HALF))
    scratch += [pltpu.SemaphoreType.DMA((12,))] * 3 + [pltpu.SemaphoreType.DMA((36,))] * 2
    return pl.pallas_call(
        scatter_kernel,
        out_shape=jax.ShapeDtypeStruct((SHARD, WIDTH), FLOAT),
        in_specs=[pl.BlockSpec(memory_space=pl.ANY)],
        out_specs=pl.BlockSpec(memory_space=pltpu.VMEM),
        scratch_shapes=scratch,
        compiler_params=pltpu.CompilerParams(
            collective_id=1, has_side_effects=True, vmem_limit_bytes=60 * 2**20
        ),
    )(grads.reshape(4, 2, 4, 2, 2, SHARD, WIDTH))


def exchange_kernel(src_ref, dst_ref, send_sem, recv_sem, own_sem):
    me = lax.axis_index("hid")
    tok = lax.axis_index("tok")
    barrier = pltpu.get_barrier_semaphore()
    for step in range(1, 8):
        pl.semaphore_signal(
            barrier, inc=1, device_id=(tok, lax.rem(me + step, 8)), device_id_type=MESH
        )
    own = pltpu.make_async_copy(src_ref.at[me], dst_ref.at[me], own_sem)
    own.start()
    pl.semaphore_wait(barrier, 7)
    copies = []
    for step in range(1, 8):
        target = lax.rem(me + step, 8)
        copy = pltpu.make_async_remote_copy(
            src_ref=src_ref.at[target], dst_ref=dst_ref.at[me],
            send_sem=send_sem.at[step - 1], recv_sem=recv_sem.at[step - 1],
            device_id=(tok, target), device_id_type=MESH,
        )
        copy.start()
        copies.append(copy)
    own.wait()
    for copy in copies:
        copy.wait()


def exchange(blocks, number):
    return pl.pallas_call(
        exchange_kernel,
        out_shape=jax.ShapeDtypeStruct(blocks.shape, blocks.dtype),
        in_specs=[pl.BlockSpec(memory_space=pl.ANY)],
        out_specs=pl.BlockSpec(memory_space=pl.ANY),
        scratch_shapes=[
            pltpu.SemaphoreType.DMA((7,)),
            pltpu.SemaphoreType.DMA((7,)),
            pltpu.SemaphoreType.DMA,
        ],
        compiler_params=pltpu.CompilerParams(collective_id=number, has_side_effects=True),
    )(blocks)


def weight_grad_kernel(
    h1_ref, g1_ref, h2_ref, mem_ref, g2_ref, h3_ref, cot_ref,
    dqkv_ref, o1_ref, dq2_ref, dkv2_ref, o2_ref, dgu_ref, hid_ref, pad_ref,
    out_ref,
):
    def put(at, left, right):
        value = dot(left[...], right[0])
        out_ref[0, :, at : at + value.shape[1]] = value.astype(HALF)

    put(0, h1_ref, dqkv_ref)
    put(256, g1_ref, o1_ref)
    put(384, h2_ref, dq2_ref)
    put(512, mem_ref, dkv2_ref)
    put(640, g2_ref, o2_ref)
    put(768, h3_ref, dgu_ref)
    value = dot(cot_ref[...], hid_ref[0])
    out_ref[0, :, 1536:1792] = value[:, :256].astype(HALF)
    out_ref[0, :, 1792:1920] = (value[:, 256:] + pad_ref[0]).astype(HALF)


def weight_grads(lefts, rights, pads):
    return pl.pallas_call(
        weight_grad_kernel,
        grid=(8,),
        out_shape=jax.ShapeDtypeStruct((8, 1024, WIDTH), HALF),
        in_specs=[pl.BlockSpec(left.shape, lambda j: (0, 0)) for left in lefts]
        + [
            pl.BlockSpec((1,) + right.shape[1:], lambda j: (j, 0, 0))
            for right in rights + [pads]
        ],
        out_specs=pl.BlockSpec((1, 1024, WIDTH), lambda j: (j, 0, 0)),
        compiler_params=pltpu.CompilerParams(vmem_limit_bytes=56 * 2**20),
    )(*lefts, *rights, pads)


def rms_norm(row_vals, gain_vec):
    return (
        row_vals * lax.rsqrt(jnp.mean(row_vals * row_vals, axis=-1, keepdims=True) + EPS) * gain_vec
    )


def norm_back(row_vals, gain_vec, gradient):
    _, pullback = jax.vjp(rms_norm, row_vals, gain_vec)
    return pullback(gradient)


def spread_cols(rows, weights):
    return jnp.einsum("rd,jdc->jrc", rows, weights, preferred_element_type=FLOAT)


def join_cols(blocks, weights):
    return jnp.einsum("jrc,jdc->rd", blocks, weights, preferred_element_type=FLOAT)


def from_windows(sums):
    sums = sums.reshape(-1, 2, PAIR)
    tail = jnp.concatenate([sums[1:, :, TILE:], jnp.zeros((1, 2, TILE), FLOAT)], axis=0)
    return (sums[:, :, :TILE] + tail).transpose(1, 0, 2).reshape(2, -1)


def local(
    tokens, memory, cotangent, norm1, w_query, w_key, w_value, w_out, rel_bias, norm2,
    cross_query, cross_key, cross_value, cross_out, norm3, w_gate, w_up, w_down,
    doc_lengths, memory_slot, enc_lengths, rel_bucket,
):
    widen = ((0, 0), (0, FF_PAD - w_gate.shape[1]))
    core = lax.rem(lax.axis_index("tok"), 2)
    hid = lax.axis_index("hid")
    packed = jnp.concatenate(
        [
            w_query, w_key, w_value, w_out.T, cross_query, cross_key, cross_value, cross_out.T,
            jnp.pad(w_gate, widen), jnp.pad(w_up, widen), jnp.pad(w_down.T, widen),
        ],
        axis=1,
    )
    norms = jnp.stack([norm1, norm2, norm3])
    blank = jnp.zeros_like(norms)
    norms = jnp.where(
        core == 0,
        jnp.concatenate([norms, blank], axis=1),
        jnp.concatenate([blank, norms], axis=1),
    )
    small = jnp.concatenate(
        [norms, jnp.broadcast_to(rel_bias.reshape(4, 1), (4, 128)), jnp.zeros((9, 128), HALF)]
    )
    tile_buckets = rel_bucket.reshape(-1, TILE)
    before = jnp.concatenate([tile_buckets[:1], tile_buckets[:-1]])
    buckets = jnp.pad(jnp.concatenate([tile_buckets, before], axis=1), ((0, 2), (0, 0)))
    (
        wf, wa, gains, windows, h_one, h_two, qkv, kv_two, o_one, o_one_rows, lse_one, x_one, q_two
    ) = forward(packed, small, tokens, memory, doc_lengths, buckets)
    wa = wa.reshape(8, 16 * SHARD, 768)
    wf = wf.reshape(8, 16 * SHARD, 1152)
    gain_one, gain_two = gains[0], gains[1]
    onehot = (
        rel_bucket[:, None] == jnp.arange(32, dtype=jnp.int32)[None, :]
    ).astype(FLOAT)
    w_qkv, w_o1, w_q2, w_kv2 = (
        wa[:, :, 0:256], wa[:, :, 256:384], wa[:, :, 384:512], wa[:, :, 512:640]
    )
    rows = tokens.shape[0]
    group_rows = rows * 8
    residual = tokens.astype(FLOAT)
    o_two, lse_two = cross_forward(doc_lengths, memory_slot, enc_lengths, q_two, kv_two)
    o_two_rows, mixed, h_three, hidden, d_gate_up, d_rows, d_out, d_norm3 = middle(
        o_two, x_one, cotangent, gains, wa, wf
    )
    d_norm3 = d_norm3[0]
    g_two = d_rows.astype(HALF)
    dq_two, dkv_two = cross_backward(
        doc_lengths, memory_slot, enc_lengths, q_two, kv_two, d_out, o_two, lse_two
    )
    dq_two = exchange(dq_two.reshape(8, rows, 128), 8)
    dkv_two = exchange(dkv_two.reshape(8, -1, 128), 9)
    d_memory = join_cols(dkv_two, w_kv2)
    d_inner, d_norm2 = norm_back(x_one, gain_two, join_cols(dq_two, w_q2))
    d_rows = d_rows + d_inner
    g_one = d_rows.astype(HALF)
    d_out = exchange(spread_cols(g_one, w_o1).astype(HALF), 10).reshape(group_rows, 128)
    dqkv, diagonals = self_backward(doc_lengths, qkv, windows, d_out, o_one, lse_one)
    dqkv = exchange(dqkv.reshape(8, rows, 256), 11)
    d_inner, d_norm1 = norm_back(residual, gain_one, join_cols(dqkv, w_qkv))
    d_tokens = d_rows + d_inner

    d_table = jnp.dot(onehot.T, from_windows(diagonals).T, precision=HIGH)
    d_table = jnp.pad(d_table.reshape(16, 2, 2), ((0, 0), (0, SHARD - 2), (0, 0)))
    d_table = d_table.reshape(1, 16 * SHARD, 2)
    owned = (jnp.arange(8, dtype=jnp.int32) == hid)[:, None, None]
    norms = jnp.stack([d_norm1, d_norm2, d_norm3], axis=1)
    pads = jnp.concatenate(
        [
            jnp.broadcast_to(norms[None], (8,) + norms.shape),
            jnp.where(owned, d_table, 0.0),
        ],
        axis=2,
    )
    pads = jnp.pad(pads, ((0, 0), (0, 0), (96, 27)))
    grads = weight_grads(
        [
            left.T for left in (h_one, g_one, h_two, memory, g_two, h_three, cotangent)
        ],
        [
            dqkv, o_one_rows, dq_two, dkv_two, o_two_rows,
            d_gate_up, hidden,
        ],
        pads,
    )
    shard = scatter_grads(grads)
    return (
        mixed,
        d_tokens,
        d_memory,
        shard[:, PAD_AT],
        shard[:, 0:128],
        shard[:, 128:192],
        shard[:, 192:256],
        shard[:, 256:384].T,
        shard[:2, PAD_AT + 3 : PAD_AT + 5],
        shard[:, PAD_AT + 1],
        shard[:, 384:512],
        shard[:, 512:576],
        shard[:, 576:640],
        shard[:, 640:768].T,
        shard[:, PAD_AT + 2],
        shard[:, 768:1120],
        shard[:, 1152:1504],
        shard[:, 1536:1888].T,
    )


def solution(mesh):
    return jax.shard_map(
        local,
        mesh=mesh,
        in_specs=(
            P(("tok", "hid"), None),
            P(("tok", "hid"), None),
            P(("tok", "hid"), None),
            P("tok"),
            P("tok", "hid"),
            P("tok", "hid"),
            P("tok", "hid"),
            P("hid", "tok"),
            P("tok", "hid"),
            P("tok"),
            P("tok", "hid"),
            P("tok", "hid"),
            P("tok", "hid"),
            P("hid", "tok"),
            P("tok"),
            P("tok", "hid"),
            P("tok", "hid"),
            P("hid", "tok"),
            P("tok", None),
            P("tok", None),
            P("tok", None),
            P(),
        ),
        out_specs=(
            P(("tok", "hid"), None),
            P(("tok", "hid"), None),
            P(("tok", "hid"), None),
            P("tok"),
            P("tok", "hid"),
            P("tok", "hid"),
            P("tok", "hid"),
            P("hid", "tok"),
            P("tok", "hid"),
            P("tok"),
            P("tok", "hid"),
            P("tok", "hid"),
            P("tok", "hid"),
            P("hid", "tok"),
            P("tok"),
            P("tok", "hid"),
            P("tok", "hid"),
            P("hid", "tok"),
        ),
        check_vma=False,
    )
```

profile of v0, /device:TPU:0, one launch (start us, length us, event | category | flops | bytes accessed | tf_op | source)
XLA Modules:
  0.0 417.9 jit_solution(17341787569658531887)
XLA Ops:
  1.2 0.7 reshape.162
  6.8 0.8 pad.25
  7.6 0.8 pad.26
  8.4 0.8 pad.27
  9.2 1.6 concatenate.24.packed_ref
  10.9 1.2 copy.103
  13.4 2.0 copy.109
  15.4 2.3 copy.106
  17.7 116.2 %shard_map.349 = (bf16[4,2,4,2,2,64,1152]{6,5,4,3,2,1,0:T(8,128)(2,1)}, bf16[4,2,4,2,2,64,768]{6,5,4,3,2,1,0:T(8,128)(2,1)}, f32[8,1024]{1,0:T(8,128)}, f32[16,5...) custom-call(bf16[64,1920]{1,0:T(8,128)(2,1)} %concatenate.24.packed_, ...), custom_call_target="tpu_custom_call" | custom-call | tf_op jit(solution)/shard_map/pallas_call | solution.py:723
  133.9 1.3 multiply_reduce_fusion.2
  135.7 1.4 fusion.39
  137.2 1.1 copy-done
  138.3 1.0 copy-done.5
  139.3 12.9 %shard_map.350 = (bf16[1536,128]{1,0:T(8,128)(2,1)S(1)}, f32[8,512]{1,0:T(8,128)S(1)}) custom-call(s32[1,3]{1,0:T(1,128)S(1)} %copy-done.15, s32[1,3]{1,0:T(1,128)S(1)} %copy-done.16, s32[1,3]{1,0:T(1,128)S(1)} %copy-done.17, bf16[1536,128]{1,0:T(8,128)(2,1)S(1)} %copy-done.5, bf16[3072,128]{1,0:T(8,128)(2,1)S(1)} %copy-done), custom_call_target="tpu_custom_call" | custom-call | tf_op jit(solution)/shard_map/pallas_call | solution.py:240
  153.0 35.4 %shard_map.351 = (bf16[8,192,128]{2,1,0:T(8,128)(2,1)}, bf16[192,1024]{1,0:T(8,128)(2,1)}, bf16[192,1024]{1,0:T(8,128)(2,1)}, bf16[8,192,384]{2,1,0:T(8,128)(2,1...) custom-call(bf16[1536,128]{1,0:T(8,128)(2,1)} %copy-done.2, ...), custom_call_target="tpu_custom_call" | custom-call | tf_op jit(solution)/shard_map/pallas_call | solution.py:852
  188.4 1.0 copy-done.12
  189.4 14.5 %shard_map.352 = (bf16[1536,128]{1,0:T(8,128)(2,1)S(1)}, bf16[3072,128]{1,0:T(8,128)(2,1)S(1)}) custom-call(s32[1,3]{1,0:T(1,128)S(1)} %copy-done.15, s32[1,3]{1,0:T(1,128)S(1)} %copy-done.16, s32[1,3]{1,0:T(1,128)S(1)} %copy-done.17, bf16[1536,128]{1,0:T(8,128)(2,1)S(1)} %copy-done.6, bf16[3072,128]{1,0:T(8,128)(2,1)S(1)} %copy-done.1, ...), custom_call_target="tpu_custom_call" | custom-call | tf_op jit(solution)/shard_map/pallas_call | solution.py:316
  203.8 0.9 copy-done.8
  204.7 0.7 copy-done.10
  205.5 10.3 %shard_map.353.dq2_ref = bf16[8,192,128]{2,1,0:T(8,128)(2,1)} custom-call(bf16[8,192,128]{2,1,0:T(8,128)(2,1)} %bitcast.63), custom_call_target="tpu_custom_call" | custom-call | tf_op jit(solution)/shard_map/pallas_call | solution.py:1063
  215.8 13.7 %shard_map.357.dkv2_ref = bf16[8,384,128]{2,1,0:T(8,128)(2,1)} custom-call(bf16[8,384,128]{2,1,0:T(8,128)(2,1)} %bitcast.61), custom_call_target="tpu_custom_call" | custom-call | tf_op jit(solution)/shard_map/pallas_call | solution.py:1063
  230.0 1.0 copy.107
  231.0 1.3 copy.100
  232.3 2.0 copy.108
  234.3 2.0 copy.104
  236.4 1.0 copy.105
  237.4 2.5 multiply_reduce_fusion
  240.0 1.1 convert_bitcast_fusion
  241.1 1.0 copy-done.20
  242.1 3.0 fusion.20.src_ref
  245.1 9.3 %shard_map.354 = bf16[8,192,128]{2,1,0:T(8,128)(2,1)} custom-call(bf16[8,192,128]{2,1,0:T(8,128)(2,1)} %fusion.20.src_ref), custom_call_target="tpu_custom_call" | custom-call | tf_op jit(solution)/shard_map/pallas_call | solution.py:1063
  254.4 1.0 copy-done.4
  255.4 15.0 %shard_map.355 = (bf16[1536,256]{1,0:T(8,128)(2,1)S(1)}, f32[12,512]{1,0:T(8,128)S(1)}) custom-call(s32[1,3]{1,0:T(1,128)S(1)} %copy-done.15, bf16[1536,256]{1,0:T(8,128)(2,1)S(1)} %copy-done.7, f32[16,512]{1,0:T(8,128)S(1)} %copy-done.13, bf16[1536,128]{1,0:T(8,128)(2,1)S(1)} %bitcast.60, bf16[1536,128]{1,0:T(8,128)(2,1)S(1)} %copy-done.11, ...), custom_call_target="tpu_custom_call" | custom-call | tf_op jit(solution)/shard_map/pallas_call | solution.py:175
  270.4 0.9 copy-done.9
  271.3 12.9 %shard_map.356.dqkv_ref = bf16[8,192,256]{2,1,0:T(8,128)(2,1)} custom-call(bf16[8,192,256]{2,1,0:T(8,128)(2,1)} %bitcast.62), custom_call_target="tpu_custom_call" | custom-call | tf_op jit(solution)/shard_map/pallas_call | solution.py:1063
  285.1 3.9 fusion.28
  289.0 3.8 fusion.8
  293.2 1.2 copy.115
  294.5 2.7 copy.114
  297.1 5.3 %pad.30.pad_ref = f32[8,1024,128]{2,1,0:T(8,128)} pad(f32[8,1024,5]{2,1,0:T(8,128)} %copy.114, f32[]{:T(128)} %constant.29.clone.1), padding=0_0x0_0x96_27 | pad | bytes 4358148 | tf_op jit(solution)/shard_map/jit(_pad)/pad | solution.py:1213
  302.4 20.1 %shard_map.358 = bf16[8,1024,1920]{2,1,0:T(8,128)(2,1)} custom-call(bf16[1024,192]{1,0:T(8,128)(2,1)} %bitcast.75, bf16[1024,192]{1,0:T(8,128)(2,1)} %get-tuple-element.151.g1_ref, bf16[1024,192]{1,0:T(8,128)(2,1)} %bitcast.76, bf16[1024,384]{1,0:T(8,128)(2,1)} %bitcast.71, bf16[1024,192]{1,0:T(8,128)(2,1)} %bitcast.73, bf16[1024,192]{1,0:T(8,128)(2,1)} %bitcast.74, ...), custom_call_target="tpu_custom_call" | custom-call | tf_op jit(solution)/shard_map/pallas_call | solution.py:1098
  322.5 87.0 %shard_map.359 = f32[64,1920]{1,0:T(8,128)} custom-call(bf16[4,2,4,2,2,64,1920]{6,5,4,3,2,1,0:T(8,128)(2,1)} %bitcast.64), custom_call_target="tpu_custom_call" | custom-call | tf_op jit(solution)/shard_map/pallas_call | solution.py:1024
  409.5 1.3 slice.106
  410.8 1.6 slice_reduce_fusion
  412.4 1.5 slice_bitcast_fusion.1
  413.9 1.6 fusion.38
  415.4 1.7 slice_bitcast_fusion
  417.1 0.7 copy.126
  (102 shorter events, 9.7 us)
Async XLA Ops:
  0.7 136.5 %copy-start.15 = (s32[1,3]{1,0:T(1,128)S(1)}, s32[1,3]{1,0:T(1,128)}, u32[]{:S(2)}) copy-start(s32[1,3]{1,0:T(1,128)} %len_ref.7) | copy-start | bytes 40
  0.7 136.5 %copy-start.17 = (s32[1,3]{1,0:T(1,128)S(1)}, s32[1,3]{1,0:T(1,128)}, u32[]{:S(2)}) copy-start(s32[1,3]{1,0:T(1,128)} %enc_ref.3) | copy-start | bytes 40
  0.7 136.5 %copy-start.16 = (s32[1,3]{1,0:T(1,128)S(1)}, s32[1,3]{1,0:T(1,128)}, u32[]{:S(2)}) copy-start(s32[1,3]{1,0:T(1,128)} %slot_ref.3) | copy-start | bytes 40
  12.2 0.6 copy-start.29
  135.2 2.0 copy-start.31
  137.2 1.1 copy-start
  138.3 1.0 copy-start.5
  152.2 0.7 copy-start.2
  152.9 35.4 %copy-start.1 = (bf16[3072,128]{1,0:T(8,128)(2,1)S(1)}, bf16[3072,128]{1,0:T(8,128)(2,1)}, u32[]{:S(2)}) copy-start(bf16[3072,128]{1,0:T(8,128)(2,1)} %get-tuple-element.46.kv_ref) | copy-start | bytes 2359300
  153.0 35.4 %copy-start.3 = (bf16[1536,128]{1,0:T(8,128)(2,1)S(1)}, bf16[1536,128]{1,0:T(8,128)(2,1)}, u32[]{:S(2)}) copy-start(bf16[1536,128]{1,0:T(8,128)(2,1)} %copy-done.2) | copy-start | bytes 1179652
  153.0 35.4 %copy-start.6 = (bf16[1536,128]{1,0:T(8,128)(2,1)S(1)}, bf16[1536,128]{1,0:T(8,128)(2,1)}, u32[]{:S(2)}) copy-start(bf16[1536,128]{1,0:T(8,128)(2,1)} %get-tuple-element.45.q_ref) | copy-start | bytes 1179652
  153.0 76.6 %copy-start.18 = (f32[192,1024]{1,0:T(8,128)S(1)}, f32[192,1024]{1,0:T(8,128)}, u32[]{:S(2)}) copy-start(f32[192,1024]{1,0:T(8,128)} %get-tuple-element.48.x1_ref) | copy-start | bytes 2359300
  188.4 1.0 copy-start.12
  189.4 40.6 %copy-start.22 = (f32[192,1024]{1,0:T(8,128)S(1)}, f32[192,1024]{1,0:T(8,128)}, u32[]{:S(2)}) copy-start(f32[192,1024]{1,0:T(8,128)} %get-tuple-element.53) | copy-start | bytes 2359300
  203.8 0.9 copy-start.8
  204.7 0.7 copy-start.10
  229.6 7.8 %copy-start.24 = (bf16[8,192,128]{2,1,0:T(8,128)(2,1)S(1)}, bf16[8,192,128]{2,1,0:T(8,128)(2,1)}, u32[]{:S(2)}) copy-start(bf16[8,192,128]{2,1,0:T(8,128)(2,1)} %shard_map.353.dq2_ref) | copy-start | bytes 1179652
  229.6 7.8 %copy-start.33 = (f32[192]{0:T(256)S(1)}, f32[192]{0:T(256)}, u32[]{:S(2)}) copy-start(f32[192]{0:T(256)} %fusion.35) | copy-start | bytes 2308
  229.9 6.4 %copy-start.25 = (bf16[192,1024]{1,0:T(8,128)(2,1)S(1)}, bf16[192,1024]{1,0:T(8,128)(2,1)}, u32[]{:S(2)}) copy-start(bf16[192,1024]{1,0:T(8,128)(2,1)} %get-tuple-element.64) | copy-start | bytes 1179652
  232.3 7.6 %copy-start.32 = (f32[192]{0:T(256)S(1)}, f32[192]{0:T(256)}, u32[]{:S(2)}) copy-start(f32[192]{0:T(256)} %copy-done.31) | copy-start | bytes 2308
  232.3 7.6 %copy-start.34 = (f32[192]{0:T(256)S(1)}, f32[192]{0:T(256)}, u32[]{:S(2)}) copy-start(f32[192]{0:T(256)} %fusion.35) | copy-start | bytes 2308
  237.4 2.6 copy-start.19
  239.9 14.4 %copy-start.7 = (bf16[1536,256]{1,0:T(8,128)(2,1)S(1)}, bf16[1536,256]{1,0:T(8,128)(2,1)}, u32[]{:S(2)}) copy-start(bf16[1536,256]{1,0:T(8,128)(2,1)} %get-tuple-element.57.qkv_ref) | copy-start | bytes 2359300
  239.9 14.4 %copy-start.11 = (bf16[1536,128]{1,0:T(8,128)(2,1)S(1)}, bf16[1536,128]{1,0:T(8,128)(2,1)}, u32[]{:S(2)}) copy-start(bf16[1536,128]{1,0:T(8,128)(2,1)} %get-tuple-element.59.o_ref) | copy-start | bytes 1179652
  240.0 14.4 %copy-start.13 = (f32[16,512]{1,0:T(8,128)S(1)}, f32[16,512]{1,0:T(8,128)}, u32[]{:S(2)}) copy-start(f32[16,512]{1,0:T(8,128)} %get-tuple-element.58.win_ref) | copy-start | bytes 98308
  240.0 14.4 %copy-start.14 = (f32[8,512]{1,0:T(8,128)S(1)}, f32[8,512]{1,0:T(8,128)}, u32[]{:S(2)}) copy-start(f32[8,512]{1,0:T(8,128)} %get-tuple-element.60.lse_ref) | copy-start | bytes 49156
  241.1 1.0 copy-start.20
  241.1 43.1 %copy-start.27 = (s32[1536]{0:T(1024)S(1)}, s32[1536]{0:T(1024)}, u32[]{:S(2)}) copy-start(s32[1536]{0:T(1024)} %param.43) | copy-start | bytes 18436
  241.1 43.1 %copy-start.38 = (s32[16,2]{0,1:T(2,128)S(1)}, s32[16,2]{0,1:T(2,128)}, u32[]{:S(2)}) copy-start(s32[16,2]{0,1:T(2,128)} %multiply_add_fusion) | copy-start | bytes 388
  241.1 43.9 %copy-start.37 = (pred[8]{0:T(512)(128)(4,1)S(1)}, pred[8]{0:T(512)(128)(4,1)}, u32[]{:S(2)}) copy-start(pred[8]{0:T(512)(128)(4,1)} %iota_compare_fusion) | copy-start | bytes 28
  241.1 43.9 %copy-start.28 = (f32[1,1024]{1,0:T(1,128)S(1)}, f32[1,1024]{1,0:T(1,128)}, u32[]{:S(2)}) copy-start(f32[1,1024]{1,0:T(1,128)} %get-tuple-element.164) | copy-start | bytes 12292
  241.1 43.9 %copy-start.36 = (f32[192]{0:T(256)S(1)}, f32[192]{0:T(256)}, u32[]{:S(2)}) copy-start(f32[192]{0:T(256)} %fusion.36) | copy-start | bytes 2308
  254.4 1.0 copy-start.4
  270.4 0.9 copy-start.9
  285.1 3.9 copy-start.23
  289.0 3.9 copy-start.30
  289.0 3.9 copy-start.21
  289.0 5.4 %copy-start.35 = (f32[1,1024]{1,0:T(1,128)S(1)}, f32[1,1024]{1,0:T(1,128)}, u32[]{:S(2)}) copy-start(f32[1,1024]{1,0:T(1,128)} %get-tuple-element.70) | copy-start | bytes 12292
  322.5 94.6 %copy-start.26 = (bf16[192,1024]{1,0:T(8,128)(2,1)S(1)}, bf16[192,1024]{1,0:T(8,128)(2,1)}, u32[]{:S(2)}) copy-start(bf16[192,1024]{1,0:T(8,128)(2,1)} %get-tuple-element.186) | copy-start | bytes 1179652
where the time goes:
time: 422 us; the launch traced here: 418 us
  Pallas kernels  347 us (82%)
  local copies, waits for them, and re-layouts  49 us (12%)
  matrix products  13.8 us (3%)
  other arithmetic  6.72 us (2%)
    pallas_call x1, Pallas kernels, forward(): pl.pallas_call(forward_kernel, out_shape=(shape(places + (SHARD, 1152), H...  116 us
    pallas_call x1, Pallas kernels, scatter_grads(): pl.pallas_call(scatter_kernel, out_shape=jax.ShapeDtypeStruct((SHARD, WID...  87 us
    pallas_call x4, Pallas kernels, exchange(): pl.pallas_call(exchange_kernel, out_shape=jax.ShapeDtypeStruct(blocks.sha...  46.2 us
    pallas_call x1, Pallas kernels, middle(): pl.pallas_call(middle_kernel, out_shape=(shape((8, rows, 128), HALF), sha...  35.4 us
    pallas_call x1, Pallas kernels, weight_grads(): pl.pallas_call(weight_grad_kernel, grid=(8,), out_shape=jax.ShapeDtypeStr...  20.1 us
    unnamed x84, local copies, waits for them, and re-layouts  16.6 us
    pallas_call x1, Pallas kernels, self_backward(): pl.pallas_call(self_backward_kernel, out_shape=(jax.ShapeDtypeStruct((row...  15 us
    pallas_call x1, Pallas kernels, cross_backward(): pl.pallas_call(cross_backward_kernel, out_shape=(jax.ShapeDtypeStruct((ro...  14.5 us

commit v1 on v0

--- a/solution.py
+++ b/solution.py
@@ -113,86 +113,6 @@
     for row in range(1, 8):
         total = total + pltpu.roll(block[row : row + 1], PAIR - row, 1)
     return total
-
-
-def self_backward_kernel(
-    len_ref, qkv_ref, win_ref, do_ref, o_ref, lse_ref,
-    dqkv_ref, diag_ref,
-    keys, values, keys_t, queries, grads, deltas, bias, bias_grad, dq,
-):
-    tiles = qkv_ref.shape[0] // TILE
-    build_bias(win_ref, bias, tiles)
-    for tile in range(tiles):
-        block = qkv_ref[tile * TILE : (tile + 1) * TILE, 128:256]
-        keys[tile] = block[:, :HDIM]
-        values[tile] = block[:, HDIM:]
-        keys_t[tile] = block[:, :HDIM].astype(FLOAT).T.astype(HALF)
-    row_prepare(tiles, lambda rows: qkv_ref[rows, 0:128], do_ref, o_ref, queries, grads, deltas)
-    bias_grad[...] = jnp.zeros_like(bias_grad)
-    dq[...] = jnp.zeros_like(dq)
-    ends = doc_ends(len_ref)
-    total_rows = qkv_ref.shape[0]
-
-    @pl.loop(0, tiles)
-    def key_tile(other):
-        last = other * TILE + TILE - 1
-        key_pos = other * TILE + lax.broadcasted_iota(jnp.int32, (TILE, 1), 0)
-        stop = jnp.where(last < ends[0], ends[0], jnp.where(last < ends[1], ends[1], total_rows))
-
-        def row_tile(tile, state):
-            dk, dv = state
-            row_pos = lane_positions(tile * TILE)
-            row_start = start_of(row_pos, ends)
-            scores = dot_nt(keys[other], queries[tile]) + bias[tile - other]
-            allowed = (key_pos <= row_pos) & (key_pos >= row_start)
-            scores = jnp.where(allowed, scores, NEG)
-            weights = jnp.exp(scores - lse_ref[pl.ds(tile, 1), :])
-            d_weights = dot_nt(values[other], grads[tile])
-            d_scores = weights * (d_weights - deltas[tile])
-            bias_grad[tile - other] += d_scores
-            d_half = d_scores.astype(HALF)
-            dv = dv + dot(weights.astype(HALF), grads[tile])
-            dk = dk + dot(d_half, queries[tile])
-            dq[tile] += dot(keys_t[other], d_half)
-            return dk, dv
-
-        zero = jnp.zeros((TILE, HDIM), FLOAT)
-        dk, dv = lax.fori_loop(other, (stop - 1) // TILE + 1, row_tile, (zero, zero))
-        dqkv_ref[tile_rows(other), 128:256] = jnp.concatenate([dk, dv], axis=1).astype(HALF)
-
-    for tile in range(tiles):
-        dqkv_ref[tile * TILE : (tile + 1) * TILE, 0:128] = unstack_heads(dq[tile]).astype(HALF)
-        for head in range(2):
-            part = bias_grad[tile, :, head * TILE : (head + 1) * TILE]
-            part = jnp.concatenate([part, jnp.zeros_like(part)], axis=1)
-            diag_ref[pl.ds(tile * 2 + head, 1), :] = fold_diagonals(part)
-
-
-def self_backward(doc_lens, qkv, windows, d_out, out, lse):
-    rows = qkv.shape[0]
-    tiles = rows // TILE
-    vmem = pl.BlockSpec(memory_space=pltpu.VMEM)
-    return pl.pallas_call(
-        self_backward_kernel,
-        out_shape=(
-            jax.ShapeDtypeStruct((rows, 256), HALF),
-            jax.ShapeDtypeStruct((2 * tiles, PAIR), FLOAT),
-        ),
-        in_specs=[pl.BlockSpec(memory_space=pltpu.SMEM)] + [vmem] * 5,
-        out_specs=(vmem, vmem),
-        scratch_shapes=[
-            pltpu.VMEM((tiles, TILE, HDIM), HALF),
-            pltpu.VMEM((tiles, TILE, HDIM), HALF),
-            pltpu.VMEM((tiles, HDIM, TILE), HALF),
-            pltpu.VMEM((tiles, PAIR, HDIM), HALF),
-            pltpu.VMEM((tiles, PAIR, HDIM), HALF),
-            pltpu.VMEM((tiles, 1, PAIR), FLOAT),
-            pltpu.VMEM((tiles, TILE, PAIR), FLOAT),
-            pltpu.VMEM((tiles, TILE, PAIR), FLOAT),
-            pltpu.VMEM((tiles, HDIM, PAIR), FLOAT),
-        ],
-        compiler_params=pltpu.CompilerParams(vmem_limit_bytes=48 * 2**20),
-    )(doc_lens, qkv, windows, d_out, out, lse)
 
 
 def cross_forward_kernel(
@@ -760,12 +680,15 @@
 
 def middle_kernel(
     o2_ref, x1_ref, cot_ref, gain_ref, wa_ref, wf_ref,
-    o2r_ref, mixed_ref, h3_ref, hid_ref, dgu_ref, g2_ref, do_ref, dnorm_ref,
-    w_out, w_ff, send_do, out_acc, in_acc, load_sem, ff_sem, *sems,
+    o2r_ref, mixed_ref, g2_ref, do_ref, dnorm_ref, yff_ref, xt3_ref, xtc_ref,
+    h3, y_stage, xs3, xsc, w_out, w_ff, send_do, out_acc, in_acc, load_sem, ff_sem, y_sem, *sems,
 ):
+    torus = Torus()
     me = lax.axis_index("hid")
     rows = x1_ref.shape[0]
     barrier = greet_hid()
+    pl.semaphore_signal(barrier, inc=1, device_id=torus.sibling(), device_id_type=MESH)
+    pairs = Pairs(torus, sems[4:6])
     load = pltpu.make_async_copy(wa_ref.at[:, :, pl.ds(640, 128)], w_out, load_sem)
     load.start()
 
@@ -781,8 +704,10 @@
         lambda j: send_do.at[j], lambda j: do_ref.at[rows_at(j, rows)], sems[2:4]
     )
     o2r_ref[me] = o2_ref[rows_at(me, rows), :]
-    pl.semaphore_wait(barrier, 7)
+    split_columns(torus, cot_ref[...].astype(FLOAT), xtc_ref.at[0], xsc)
+    pl.semaphore_wait(barrier, 8)
     o2_trade.start_all()
+    copies = [pairs.send(lambda: xsc, lambda: xtc_ref.at[1])]
     load.wait()
     o2_trade.arrived()
     x_two = x1_ref[...]
@@ -793,7 +718,21 @@
     out_acc[...] = x_two
     g2_ref[...] = x_two
     in_acc[...] = jnp.zeros_like(in_acc)
-    h3_ref[...] = (x_two * scale_of(x_two) * gain_ref[2:3, :]).astype(HALF)
+    h3[...] = (x_two * scale_of(x_two) * gain_ref[2:3, :]).astype(HALF)
+    split_columns(torus, h3[...].astype(FLOAT), xt3_ref.at[0], xs3)
+    copies.append(pairs.send(lambda: xs3, lambda: xt3_ref.at[1]))
+
+    def keep(j):
+        return pltpu.make_async_copy(
+            y_stage.at[j], yff_ref.at[j, pl.ds(0, rows)], y_sem.at[0, j]
+        )
+
+    def share(j):
+        return pltpu.make_async_remote_copy(
+            src_ref=y_stage.at[j], dst_ref=yff_ref.at[j, pl.ds(rows, rows)],
+            send_sem=y_sem.at[1, j], recv_sem=y_sem.at[2, j],
+            device_id=torus.sibling(), device_id_type=MESH,
+        )
 
     @pl.loop(0, 8)
     def one_block(j):
@@ -803,7 +742,7 @@
 
         fetch(j).wait()
         slot = lax.rem(j, 2)
-        gate_up = dot(h3_ref[...], w_ff[slot, :, 0:768])
+        gate_up = dot(h3[...], w_ff[slot, :, 0:768])
         gate, up = gate_up[:, :FF_PAD], gate_up[:, FF_PAD:]
         d_hidden = dot(cot_ref[...], w_ff[slot, :, 768:1152])
         curve = 0.7978845608028654 * (gate + 0.044715 * gate * gate * gate)
@@ -813,9 +752,11 @@
             0.7978845608028654 * (1.0 + 3.0 * 0.044715 * gate * gate)
         )
         hidden = (gelu * up).astype(HALF)
-        hid_ref[j] = hidden
+        y_stage[j, :, 768:1152] = hidden
         d_both = jnp.concatenate([d_hidden * up * slope, d_hidden * gelu], axis=1).astype(HALF)
-        dgu_ref[j] = d_both
+        y_stage[j, :, 0:768] = d_both
+        keep(j).start()
+        share(j).start()
         out_acc[...] += dot_nt(hidden, w_ff[slot, :, 768:1152])
         in_acc[...] += dot_nt(d_both, w_ff[slot, :, 0:768])
 
@@ -842,6 +783,14 @@
     do_trade.arrived()
     o2_trade.finish()
     do_trade.finish()
+    for copy in copies:
+        copy.wait_recv()
+    pairs.finish()
+
+    @pl.loop(0, 8)
+    def settle(j):
+        keep(j).wait()
+        share(j).wait()
 
 
 def middle(o_two, x_one, cotangent, gains, wa, wf):
@@ -854,16 +803,20 @@
         out_shape=(
             shape((8, rows, 128), HALF),
             shape((rows, 1024), HALF),
-            shape((rows, 1024), HALF),
-            shape((8, rows, FF_PAD), HALF),
-            shape((8, rows, 2 * FF_PAD), HALF),
             shape((rows, 1024), FLOAT),
             shape((rows * 8, 128), HALF),
             shape((1, 1024), FLOAT),
+            shape((8, 2 * rows, 3 * FF_PAD), HALF),
+            shape((2, 4, 2, SHARD, rows), HALF),
+            shape((2, 4, 2, SHARD, rows), HALF),
         ),
         in_specs=[vmem] * 4 + [anywhere] * 2,
-        out_specs=(vmem,) * 8,
+        out_specs=(vmem,) * 5 + (anywhere, vmem, vmem),
         scratch_shapes=[
+            pltpu.VMEM((rows, 1024), HALF),
+            pltpu.VMEM((8, rows, 3 * FF_PAD), HALF),
+            pltpu.VMEM((4, 2, SHARD, rows), HALF),
+            pltpu.VMEM((4, 2, SHARD, rows), HALF),
             pltpu.VMEM((8, 1024, 128), HALF),
             pltpu.VMEM((2, 1024, 1152), HALF),
             pltpu.VMEM((8, rows, 128), HALF),
@@ -871,24 +824,66 @@
             pltpu.VMEM((rows, 1024), FLOAT),
             pltpu.SemaphoreType.DMA,
             pltpu.SemaphoreType.DMA((2,)),
+            pltpu.SemaphoreType.DMA((3, 8)),
         ]
-        + trade_sems() * 2,
+        + trade_sems() * 2
+        + [pltpu.SemaphoreType.DMA((2,))] * 2,
         compiler_params=pltpu.CompilerParams(
             collective_id=2, has_side_effects=True, vmem_limit_bytes=56 * 2**20
         ),
     )(o_two, x_one, cotangent, gains, wa, wf)
 
 
-def scatter_kernel(
-    g_ref, out_ref, acc, core_in, *rest
-):
-    buffers = rest[:18]
-    core_send, core_recv, load_sem, send_sem, recv_sem = rest[18:]
-    torus = Torus()
-    barrier = torus.greet()
-    pl.semaphore_wait(barrier, 7)
-
-    def add_blocks(place, whole, rows, cut, sources):
+class Remote:
+    def __init__(self, src, dst, sems, at, target):
+        self.src, self.dst, self.sems, self.at, self.target = src, dst, sems, at, target
+
+    def copy(self):
+        return pltpu.make_async_remote_copy(
+            src_ref=self.src(), dst_ref=self.dst(),
+            send_sem=self.sems[0].at[self.at], recv_sem=self.sems[1].at[self.at],
+            device_id=self.target(), device_id_type=MESH,
+        )
+
+    def start(self):
+        self.copy().start()
+
+    def wait_recv(self):
+        self.copy().wait_recv()
+
+    def wait_send(self):
+        self.copy().wait_send()
+
+
+class Drain:
+    def __init__(self, torus, acc, out_ref, cuts, orders, halves, fill, buffers, sems):
+        self.torus, self.acc, self.out_ref, self.fill = torus, acc, out_ref, fill
+        self.cuts, self.orders, self.halves = cuts, orders, halves
+        self.buffers, self.sems = buffers, sems
+        self.rows = (0, acc.shape[4])
+        self.sends, self.last = [], {}
+
+    def plan(self, stage):
+        for part, cut in enumerate(self.cuts):
+            first = (stage * len(self.cuts) + part) * 2
+            got, final = self.buffers[first : first + 2]
+            yield part, cut, self.orders[part][stage], self.orders[part][:stage], got, final
+
+    def view(self, place, whole, rows, cut):
+        return self.acc.at[block_index(place, whole) + (pl.ds(*rows), pl.ds(*cut))]
+
+    def send(self, axis, hops, step, whole, rows, cut, buffer, slot):
+        copy = Remote(
+            lambda: self.view(self.torus.moved(axis, hops), whole, rows, cut),
+            lambda: buffer.at[slot],
+            self.sems, len(self.sends),
+            lambda: self.torus.neighbour(axis, step),
+        )
+        copy.start()
+        self.sends.append(copy)
+        return copy
+
+    def add(self, place, whole, rows, cut, sources):
         dims = whole_dims(whole)
         count = 1
         for dim in dims:
@@ -906,232 +901,553 @@
                 for entry in block_index(place, whole)
             )
             where = at + (pl.ds(*rows), pl.ds(*cut))
-            total = acc[where].astype(FLOAT)
-            for source in sources:
-                total = total + source(at, tuple(index)).astype(FLOAT)
-            acc[where] = total.astype(acc.dtype)
+            total = self.acc[where].astype(FLOAT)
+            for buffer, slot in sources:
+                total = total + buffer[(slot,) + tuple(index)].astype(FLOAT)
+            self.acc[where] = total.astype(self.acc.dtype)
 
         if count == 1:
             one(jnp.int32(0))
         else:
             pl.loop(0, count)(one)
 
-    core_copies = {}
-    for step in (2, 1, -1, 0):
-        for part, cut in enumerate(CUTS):
-            axis, whole = ORDERS[part][2], ORDERS[part][:2]
-            at = block_index(torus.moved(axis, step), whole)
-            cols = (slice(None), pl.ds(*cut))
-            number = len(core_copies)
-            remote = pltpu.make_async_remote_copy(
-                src_ref=g_ref.at[at + (1 - torus.core,) + cols],
-                dst_ref=core_in.at[at + cols],
-                send_sem=core_send.at[number],
-                recv_sem=core_recv.at[number],
-                device_id=torus.sibling(),
-                device_id_type=MESH,
+    def begin(self, stage):
+        torus = self.torus
+        for part, cut, axis, whole, got, _ in self.plan(stage):
+            across = torus.moved(axis, 2)
+            if stage == 2:
+                self.fill(part, across, axis)
+            self.last[part] = [
+                self.send(axis, 2, 1 - 2 * slot, whole, rows, cut, got, slot)
+                for slot, rows in enumerate(self.halves)
+            ]
+
+    def fill_rest(self):
+        for part, cut, axis, whole, _, _ in self.plan(2):
+            for step in (1, -1, 0):
+                self.fill(part, self.torus.moved(axis, step), axis)
+
+    def turn(self, stage):
+        torus = self.torus
+        for part, cut, axis, whole, got, final in self.plan(stage):
+            copies = []
+            for slot, step in enumerate((1, -1)):
+                place = torus.moved(axis, step)
+                if slot < len(self.halves):
+                    self.last[part][slot].wait_recv()
+                    self.add(place, whole, self.halves[slot], cut, [(got, slot)])
+                copies.append(self.send(axis, step, step, whole, self.rows, cut, final, slot))
+            self.last[part] = copies
+
+    def settle(self, stage):
+        for part, cut, axis, whole, _, final in self.plan(stage):
+            for copy in self.last[part]:
+                copy.wait_recv()
+            if stage > 0:
+                self.add(self.torus.pos, whole, self.rows, cut, [(final, 0), (final, 1)])
+            else:
+                mine = self.acc[block_index(self.torus.pos, "") + (slice(None), pl.ds(*cut))]
+                self.out_ref[:, pl.ds(*cut)] = (
+                    mine.astype(FLOAT) + final[0].astype(FLOAT) + final[1].astype(FLOAT)
+                )
+
+    def finish(self):
+        for copy in self.sends:
+            copy.wait_send()
+
+
+def drain_scratch(cuts, orders, halves, rows, dtype):
+    width = sum(cut[1] for cut in cuts)
+    scratch = [pltpu.VMEM((4, 2, 4, 2, rows, width), dtype)]
+    for stage in range(3):
+        for part, cut in enumerate(cuts):
+            dims = whole_dims(orders[part][:stage])
+            scratch.append(pltpu.VMEM((len(halves),) + dims + (halves[0][1], cut[1]), dtype))
+            scratch.append(pltpu.VMEM((2,) + dims + (rows, cut[1]), dtype))
+    count = len(cuts) * 3 * (2 + len(halves))
+    return scratch + [pltpu.SemaphoreType.DMA((count,))] * 2
+
+
+class Pairs:
+    def __init__(self, torus, sems):
+        self.torus, self.sems, self.log = torus, sems, []
+
+    def send(self, src, dst):
+        copy = Remote(src, dst, self.sems, len(self.log), self.torus.sibling)
+        copy.start()
+        self.log.append(copy)
+        return copy
+
+    def finish(self):
+        for copy in self.log:
+            copy.wait_send()
+
+
+def split_columns(torus, value, mine_ref, other_ref):
+    turned = value.T.astype(HALF).reshape(4, 2, 2, SHARD, value.shape[0])
+    first = torus.core == 0
+    mine_ref[...] = jnp.where(first, turned[:, :, 0], turned[:, :, 1])
+    other_ref[...] = jnp.where(first, turned[:, :, 1], turned[:, :, 0])
+
+
+def fill_product(acc, first, width, turned, right, place, axis):
+    cols = pl.ds(first, width)
+
+    def block(j, pick, count):
+        total = None
+        for side in range(2):
+            left = pick(side).reshape(count, turned.shape[-1])
+            value = dot(left, right(j, side))
+            total = value if total is None else total + value
+        return total.astype(HALF)
+
+    if axis == "x":
+        xlo, xhi = lax.rem(place["x"], 2), place["x"] // 2
+
+        @pl.loop(0, 4)
+        def one_z(z):
+            value = block(z * 2 + xlo, lambda side: turned[side, :, xhi], 256)
+            acc[z, xlo, :, xhi, :, cols] = value.reshape(4, SHARD, width)
+
+    elif axis == "z":
+        z = place["z"]
+
+        @pl.loop(0, 2)
+        def one_x(xlo):
+            value = block(z * 2 + xlo, lambda side: turned[side], 512)
+            acc[z, xlo, :, :, :, cols] = value.reshape(4, 2, SHARD, width)
+
+    else:
+        y = place["y"]
+
+        @pl.loop(0, 8)
+        def one_j(j):
+            value = block(j, lambda side: turned[side, y], 128)
+            acc[j // 2, lax.rem(j, 2), y, :, :, cols] = value.reshape(2, SHARD, width)
+
+
+FF_CUTS = ((0, 384), (384, 384), (768, 384))
+MIX_CUTS = ((0, 128), (128, 128), (256, 256))
+QKV_CUTS = ((0, 128), (128, 128))
+LAST_CUTS = ((0, 128),)
+QKV_ORDERS = (ORDERS[0], ORDERS[2])
+LAST_ORDERS = (ORDERS[1],)
+HALVES = ((0, 32), (32, 32))
+WHOLE = ((0, 16),)
+
+
+def backward_kernel(
+    dq2_ref, dkv2_ref, g2_ref, x1_ref, tok_ref, mem_ref, h1_ref, h2_ref, o1r_ref, o2r_ref,
+    gain_ref, wa_ref, yff_ref, xt3_ref, xtc_ref, qkv_ref, win_ref, o1_ref, lse_ref, len_ref,
+    bucket_ref, dnorm3_ref,
+    dtok_ref, dmem_ref, ff_out, mix_out, qkv_out, last_out,
+    *rest,
+):
+    rest = list(rest)
+
+    def take(count):
+        taken = rest[:count]
+        del rest[:count]
+        return taken
+
+    y_o1, y_o2, y_q2, y_kv2, y_qkv = take(5)
+    xt_h1, xt_h2, xt_mem, xt_g1, xt_g2 = take(5)
+    xs_h1, xs_h2, xs_mem, xs_g1, xs_g2 = take(5)
+    g1_half, send_do, do_ref, dqkv_ref, last_own, last_in, norms = take(7)
+    ff_scratch, mix_scratch, qkv_scratch, last_scratch = take(19), take(19), take(13), take(7)
+    local_sem = rest.pop(0)
+    sems = rest
+    ff_sems, mix_sems, qkv_sems, last_sems = sems[0:2], sems[2:4], sems[4:6], sems[6:8]
+    pair_sems, trade_sem = sems[8:10], sems[10:18]
+
+    torus = Torus()
+    me = lax.axis_index("hid")
+    rows, mem_rows = tok_ref.shape[0], mem_ref.shape[0]
+    tiles = qkv_ref.shape[0] // TILE
+    barrier, count = greet_all(torus)
+    owns = [
+        pltpu.make_async_copy(o1r_ref, y_o1.at[:, pl.ds(0, rows)], local_sem.at[0]),
+        pltpu.make_async_copy(o2r_ref, y_o2.at[:, pl.ds(0, rows)], local_sem.at[1]),
+    ]
+    for own in owns:
+        own.start()
+    dq2_trade = Trade(
+        lambda j: dq2_ref.at[rows_at(j, rows)], lambda j: y_q2.at[j, pl.ds(0, rows)],
+        trade_sem[0:2],
+    )
+    dkv2_trade = Trade(
+        lambda j: dkv2_ref.at[rows_at(j, mem_rows)], lambda j: y_kv2.at[j, pl.ds(0, mem_rows)],
+        trade_sem[2:4],
+    )
+    do_trade = Trade(
+        lambda j: send_do.at[j], lambda j: do_ref.at[rows_at(j, rows)], trade_sem[4:6]
+    )
+    dqkv_trade = Trade(
+        lambda j: dqkv_ref.at[rows_at(j, rows)], lambda j: y_qkv.at[j, pl.ds(0, rows)],
+        trade_sem[6:8],
+    )
+    pairs = Pairs(torus, pair_sems)
+
+    def share(buffer, size):
+        return pairs.send(
+            lambda: buffer.at[:, pl.ds(0, size)], lambda: buffer.at[:, pl.ds(size, size)]
+        )
+
+    def fill_mix(part, place, axis):
+        def right(ref, size):
+            return lambda j, side: ref[j, side * size : (side + 1) * size, :]
+
+        if part == 0:
+            fill_product(mix_scratch[0], 0, 128, xt_g1, right(y_o1, rows), place, axis)
+        elif part == 1:
+            fill_product(mix_scratch[0], 128, 128, xt_h2, right(y_q2, rows), place, axis)
+        else:
+            fill_product(mix_scratch[0], 256, 128, xt_mem, right(y_kv2, mem_rows), place, axis)
+            fill_product(mix_scratch[0], 384, 128, xt_g2, right(y_o2, rows), place, axis)
+
+    def fill_qkv(part, place, axis):
+        first = part * 128
+
+        def right(j, side):
+            return y_qkv[j, side * rows : (side + 1) * rows, first : first + 128]
+
+        fill_product(qkv_scratch[0], first, 128, xt_h1, right, place, axis)
+
+    drain_ff = Drain(
+        torus, ff_scratch[0], ff_out, FF_CUTS, ORDERS, HALVES, None, ff_scratch[1:], ff_sems
+    )
+    drain_mix = Drain(
+        torus, mix_scratch[0], mix_out, MIX_CUTS, ORDERS, HALVES, fill_mix, mix_scratch[1:],
+        mix_sems,
+    )
+    drain_qkv = Drain(
+        torus, qkv_scratch[0], qkv_out, QKV_CUTS, QKV_ORDERS, HALVES, fill_qkv, qkv_scratch[1:],
+        qkv_sems,
+    )
+    drain_last = Drain(
+        torus, last_scratch[0], last_out, LAST_CUTS, LAST_ORDERS, WHOLE,
+        lambda part, place, axis: None, last_scratch[1:], last_sems,
+    )
+
+    y_q2[me, 0:rows] = dq2_ref[rows_at(me, rows), :]
+    y_kv2[me, 0:mem_rows] = dkv2_ref[rows_at(me, mem_rows), :]
+    pl.semaphore_wait(barrier, count)
+    dq2_trade.start_all()
+    dkv2_trade.start_all()
+
+    def load_ff(yff):
+        load = pltpu.make_async_copy(yff_ref, yff, local_sem.at[2])
+        load.start()
+        split_columns(torus, g2_ref[...], xt_g2.at[0], xs_g2)
+        split_columns(torus, h2_ref[...].astype(FLOAT), xt_h2.at[0], xs_h2)
+        load.wait()
+
+        def fill(part, place, axis):
+            first = part * 384
+
+            def right(j, side):
+                return yff[j, side * rows : (side + 1) * rows, first : first + 384]
+
+            turned = xtc_ref if part == 2 else xt3_ref
+            fill_product(ff_scratch[0], first, 384, turned, right, place, axis)
+
+        drain_ff.fill = fill
+        drain_ff.begin(2)
+        drain_ff.fill_rest()
+
+    pl.run_scoped(load_ff, pltpu.VMEM((8, 2 * rows, 1152), HALF))
+    pair_g2 = pairs.send(lambda: xs_g2, lambda: xt_g2.at[1])
+    pair_h2 = pairs.send(lambda: xs_h2, lambda: xt_h2.at[1])
+
+    def inner(w_in, w_out, dmem):
+        loads = [
+            pltpu.make_async_copy(wa_ref.at[:, :, pl.ds(384, 256)], w_in, local_sem.at[2]),
+            pltpu.make_async_copy(wa_ref.at[:, :, pl.ds(256, 128)], w_out, local_sem.at[3]),
+        ]
+        for load in loads:
+            load.start()
+        split_columns(torus, mem_ref[...].astype(FLOAT), xt_mem.at[0], xs_mem)
+        split_columns(torus, h1_ref[...].astype(FLOAT), xt_h1.at[0], xs_h1)
+        pair_mem = pairs.send(lambda: xs_mem, lambda: xt_mem.at[1])
+        pair_h1 = pairs.send(lambda: xs_h1, lambda: xt_h1.at[1])
+        for own in owns:
+            own.wait()
+        pair_y = [
+            share(y, size) for y, size in ((y_o1, rows), (y_o2, rows))
+        ]
+        for load in loads:
+            load.wait()
+        dq2_trade.arrived()
+        pair_q2 = share(y_q2, rows)
+        total = jnp.zeros((rows, 1024), FLOAT)
+        for pair in range(4):
+            left = [y_q2[2 * pair + side, 0:rows] for side in range(2)]
+            right = [w_in[2 * pair + side, :, 0:128] for side in range(2)]
+            total = total + dot_nt(
+                jnp.concatenate(left, axis=1), jnp.concatenate(right, axis=1)
             )
-            remote.start()
-            here = pltpu.make_async_copy(
-                g_ref.at[at + (torus.core,) + cols], acc.at[at + cols], load_sem.at[number]
-            )
-            here.start()
-            core_copies[step, part] = (remote, here)
-
-    def core_sum(step, part):
-        remote, here = core_copies[step, part]
-        remote.wait_recv()
-        here.wait()
-        axis, whole, cut = ORDERS[part][2], ORDERS[part][:2], CUTS[part]
-        add_blocks(
-            torus.moved(axis, step), whole, (0, SHARD), cut,
-            [lambda at, index: core_in[at + (slice(None), pl.ds(*cut))]],
+        d_inner, d_gain = norm_backward(x1_ref[...], gain_ref[1:2, :], total)
+        norms[1:2, :] = d_gain
+        norms[2:3, :] = dnorm3_ref[...]
+        g_one = g2_ref[...] + d_inner
+        dtok_ref[...] = g_one
+        g1_half[...] = g_one.astype(HALF)
+
+        def one(step, j, remote):
+            value = dot(g1_half[...], w_out[j]).astype(HALF)
+
+            @pl.when(remote)
+            def _():
+                send_do[j] = value
+                do_trade.start(step)
+
+            @pl.when(jnp.logical_not(remote))
+            def _():
+                do_ref[rows_at(me, rows), :] = value
+
+        each_target(one)
+        drain_ff.turn(2)
+        split_columns(torus, dtok_ref[...], xt_g1.at[0], xs_g1)
+        pair_g1 = pairs.send(lambda: xs_g1, lambda: xt_g1.at[1])
+        dkv2_trade.arrived()
+        pair_kv2 = share(y_kv2, mem_rows)
+        for pair in range(4):
+            left = [y_kv2[2 * pair + side, 0:mem_rows] for side in range(2)]
+            right = [w_in[2 * pair + side, :, 128:256] for side in range(2)]
+            value = dot_nt(jnp.concatenate(left, axis=1), jnp.concatenate(right, axis=1))
+            dmem[...] = value if pair == 0 else dmem[...] + value
+        store = pltpu.make_async_copy(dmem, dmem_ref, local_sem.at[2])
+        store.start()
+        for copy in [pair_g2, pair_h2, pair_mem, pair_q2, pair_g1, pair_kv2] + pair_y:
+            copy.wait_recv()
+        drain_mix.begin(2)
+        drain_mix.fill_rest()
+        pair_h1.wait_recv()
+        store.wait()
+
+    pl.run_scoped(
+        inner,
+        pltpu.VMEM((8, 1024, 256), HALF),
+        pltpu.VMEM((8, 1024, 128), HALF),
+        pltpu.VMEM((mem_rows, 1024), FLOAT),
+    )
+    drain_ff.settle(2)
+    drain_ff.begin(1)
+    do_trade.arrived()
+
+    def self_attention(keys, values, keys_t, queries, grads, deltas, bias, bias_grad, dq):
+        build_bias(win_ref, bias, tiles)
+        for tile in range(tiles):
+            block = qkv_ref[tile * TILE : (tile + 1) * TILE, 128:256]
+            keys[tile] = block[:, :HDIM]
+            values[tile] = block[:, HDIM:]
+            keys_t[tile] = block[:, :HDIM].astype(FLOAT).T.astype(HALF)
+        row_prepare(
+            tiles, lambda at: qkv_ref[at, 0:128], do_ref, o1_ref, queries, grads, deltas
         )
-
-    sends = []
-
-    def send(src, dst, target):
-        at = len(sends)
-        copy = pltpu.make_async_remote_copy(
-            src_ref=src, dst_ref=dst, send_sem=send_sem.at[at], recv_sem=recv_sem.at[at],
-            device_id=target, device_id_type=MESH,
-        )
-        copy.start()
-        sends.append(copy)
-        return copy
-
-    def view(place, whole, rows, cut):
-        return acc.at[block_index(place, whole) + (pl.ds(*rows), pl.ds(*cut))]
-
-    def landed(buffer, slot):
-        return lambda at, index: buffer[(slot,) + index]
-
-    for stage in (2, 1, 0):
-        far, near = [], []
-        for part, cut in enumerate(CUTS):
-            if stage == 2:
-                core_sum(2, part)
-            axis, whole = ORDERS[part][stage], ORDERS[part][:stage]
-            buffer = buffers[(stage * 3 + part) * 2]
-            across = torus.moved(axis, 2)
-            far.append((
-                send(view(across, whole, (0, 32), cut), buffer.at[0], torus.neighbour(axis, 1)),
-                send(view(across, whole, (32, 32), cut), buffer.at[1], torus.neighbour(axis, -1)),
-            ))
-        for part, cut in enumerate(CUTS):
-            if stage == 2:
-                core_sum(1, part)
-                core_sum(-1, part)
-            axis, whole = ORDERS[part][stage], ORDERS[part][:stage]
-            got, last = buffers[(stage * 3 + part) * 2 : (stage * 3 + part) * 2 + 2]
-            pair = []
-            for slot, step, rows in ((0, 1, (0, 32)), (1, -1, (32, 32))):
-                place = torus.moved(axis, step)
-                far[part][slot].wait_recv()
-                add_blocks(place, whole, rows, cut, [landed(got, slot)])
-                pair.append(
-                    send(view(place, whole, (0, SHARD), cut), last.at[slot], torus.neighbour(axis, step))
-                )
-            near.append(pair)
-        for part, cut in enumerate(CUTS):
-            if stage == 2:
-                core_sum(0, part)
-            whole = ORDERS[part][:stage]
-            last = buffers[(stage * 3 + part) * 2 + 1]
-            near[part][0].wait_recv()
-            near[part][1].wait_recv()
-            if stage > 0:
-                add_blocks(torus.pos, whole, (0, SHARD), cut, [landed(last, 0), landed(last, 1)])
-            else:
-                mine = acc[block_index(torus.pos, "") + (slice(None), pl.ds(*cut))]
-                out_ref[:, pl.ds(*cut)] = (
-                    mine.astype(FLOAT) + last[0].astype(FLOAT) + last[1].astype(FLOAT)
-                )
-    for copy in sends:
-        copy.wait_send()
-    for remote, _ in core_copies.values():
-        remote.wait_send()
-
-
-def scatter_grads(grads):
-    scratch = [pltpu.VMEM((4, 2, 4, 2, SHARD, WIDTH), HALF)] * 2
-    for stage in range(3):
-        for part, cut in enumerate(CUTS):
-            dims = whole_dims(ORDERS[part][:stage])
-            scratch.append(pltpu.VMEM((2,) + dims + (32, cut[1]), HALF))
-            scratch.append(pltpu.VMEM((2,) + dims + (SHARD, cut[1]), HALF))
-    scratch += [pltpu.SemaphoreType.DMA((12,))] * 3 + [pltpu.SemaphoreType.DMA((36,))] * 2
+        bias_grad[...] = jnp.zeros_like(bias_grad)
+        dq[...] = jnp.zeros_like(dq)
+        ends = doc_ends(len_ref)
+
+        def key_tile(other):
+            key_pos = other * TILE + lax.broadcasted_iota(jnp.int32, (TILE, 1), 0)
+
+            def row_tile(tile, state):
+                dk, dv = state
+                row_pos = lane_positions(tile * TILE)
+                row_start = start_of(row_pos, ends)
+                scores = dot_nt(keys[other], queries[tile]) + bias[tile - other]
+                allowed = (key_pos <= row_pos) & (key_pos >= row_start)
+                scores = jnp.where(allowed, scores, NEG)
+                weights = jnp.exp(scores - lse_ref[pl.ds(tile, 1), :])
+                d_weights = dot_nt(values[other], grads[tile])
+                d_scores = weights * (d_weights - deltas[tile])
+                bias_grad[tile - other] += d_scores
+                d_half = d_scores.astype(HALF)
+                dv = dv + dot(weights.astype(HALF), grads[tile])
+                dk = dk + dot(d_half, queries[tile])
+                dq[tile] += dot(keys_t[other], d_half)
+                return dk, dv
+
+            zero = jnp.zeros((TILE, HDIM), FLOAT)
+            dk, dv = lax.fori_loop(other, tiles, row_tile, (zero, zero))
+            dqkv_ref[tile_rows(other), 128:256] = jnp.concatenate([dk, dv], axis=1).astype(HALF)
+
+        pl.loop(0, 2)(key_tile)
+        drain_ff.turn(1)
+        drain_mix.turn(2)
+        pl.loop(2, tiles)(key_tile)
+        drain_ff.settle(1)
+        drain_ff.begin(0)
+        for tile in range(tiles):
+            dqkv_ref[tile * TILE : (tile + 1) * TILE, 0:128] = unstack_heads(dq[tile]).astype(HALF)
+        dqkv_trade.start_all()
+        y_qkv[me, 0:rows] = dqkv_ref[rows_at(me, rows), :]
+        sums = []
+        for head in range(2):
+            parts = []
+            for tile in range(tiles):
+                part = bias_grad[tile, :, head * TILE : (head + 1) * TILE]
+                part = jnp.concatenate([part, jnp.zeros_like(part)], axis=1)
+                parts.append(fold_diagonals(part))
+            parts.append(jnp.zeros((8 - tiles, PAIR), FLOAT))
+            sums.append(jnp.concatenate(parts, axis=0))
+        buckets = bucket_ref[...]
+        last_own[...] = jnp.zeros_like(last_own)
+        for bucket in range(32):
+            mask = buckets == bucket
+            shard, part = bucket // 2, bucket % 2
+            for head in range(2):
+                picked = jnp.where(mask, sums[head], 0.0)
+                value = jnp.sum(jnp.sum(picked, axis=0, keepdims=True), axis=1, keepdims=True)
+                at = 3 + part * 2 + head
+                last_own[shard % 2, shard // 2, at : at + 1, :] = jnp.broadcast_to(value, (1, 128))
+
+    pl.run_scoped(
+        self_attention,
+        pltpu.VMEM((tiles, TILE, HDIM), HALF),
+        pltpu.VMEM((tiles, TILE, HDIM), HALF),
+        pltpu.VMEM((tiles, HDIM, TILE), HALF),
+        pltpu.VMEM((tiles, PAIR, HDIM), HALF),
+        pltpu.VMEM((tiles, PAIR, HDIM), HALF),
+        pltpu.VMEM((tiles, 1, PAIR), FLOAT),
+        pltpu.VMEM((tiles, TILE, PAIR), FLOAT),
+        pltpu.VMEM((tiles, TILE, PAIR), FLOAT),
+        pltpu.VMEM((tiles, HDIM, PAIR), FLOAT),
+    )
+
+    def first_inputs(w_in):
+        load = pltpu.make_async_copy(wa_ref.at[:, :, pl.ds(0, 256)], w_in, local_sem.at[2])
+        load.start()
+        drain_mix.settle(2)
+        drain_mix.begin(1)
+        drain_ff.turn(0)
+        load.wait()
+        dqkv_trade.arrived()
+        pair_qkv = share(y_qkv, rows)
+        total = jnp.zeros((rows, 1024), FLOAT)
+        for j in range(8):
+            total = total + dot_nt(y_qkv[j, 0:rows], w_in[j])
+        residual = tok_ref[...].astype(FLOAT)
+        d_inner, d_gain = norm_backward(residual, gain_ref[0:1, :], total)
+        norms[0:1, :] = d_gain
+        dtok_ref[...] += d_inner
+        return pair_qkv
+
+    pair_qkv = []
+
+    def scoped_first(w_in):
+        pair_qkv.append(first_inputs(w_in))
+
+    pl.run_scoped(scoped_first, pltpu.VMEM((8, 1024, 256), HALF))
+    for pair in range(8):
+        part = norms[0:3, pair * 128 : (pair + 1) * 128]
+        for core in range(2):
+            last_own[core, pair, 0:3, :] = part
+    pair_last = pairs.send(lambda: last_own.at[1 - torus.core], lambda: last_in)
+    pair_qkv[0].wait_recv()
+    drain_qkv.begin(2)
+    drain_qkv.fill_rest()
+    drain_mix.turn(1)
+    drain_ff.settle(0)
+    pair_last.wait_recv()
+    line = lax.broadcasted_iota(jnp.int32, (8, 16, 128), 1)
+    total = last_own[torus.core] + last_in[...]
+    shared = jnp.where(line < 3, total, 0.0)
+
+    @pl.loop(0, 8)
+    def one_j(j):
+        value = jnp.where(j == me, total, shared)
+        last_scratch[0][j // 2, lax.rem(j, 2)] = value.reshape(4, 2, 16, 128)
+
+    drain_last.begin(2)
+    drain_qkv.turn(2)
+    drain_last.turn(2)
+    drain_mix.settle(1)
+    drain_mix.begin(0)
+    drain_qkv.settle(2)
+    drain_qkv.begin(1)
+    drain_last.settle(2)
+    drain_last.begin(1)
+    drain_mix.turn(0)
+    drain_qkv.turn(1)
+    drain_last.turn(1)
+    drain_mix.settle(0)
+    drain_qkv.settle(1)
+    drain_qkv.begin(0)
+    drain_last.settle(1)
+    drain_last.begin(0)
+    drain_qkv.turn(0)
+    drain_last.turn(0)
+    drain_qkv.settle(0)
+    drain_last.settle(0)
+    for drain in (drain_ff, drain_mix, drain_qkv, drain_last):
+        drain.finish()
+    for trade in (dq2_trade, dkv2_trade, do_trade, dqkv_trade):
+        trade.finish()
+    pairs.finish()
+
+
+def backward(
+    dq2, dkv2, g2, x1, tokens, memory, h1, h2, o1r, o2r, gains, wa, yff, xt3, xtc, qkv, windows,
+    o1, lse, doc_lens, buckets, dnorm3,
+):
+    rows, mem_rows = tokens.shape[0], memory.shape[0]
+    group = rows * 8
+    vmem = pl.BlockSpec(memory_space=pltpu.VMEM)
+    smem = pl.BlockSpec(memory_space=pltpu.SMEM)
+    anywhere = pl.BlockSpec(memory_space=pl.ANY)
+    shape = jax.ShapeDtypeStruct
+    drains = [
+        drain_scratch(FF_CUTS, ORDERS, HALVES, SHARD, HALF),
+        drain_scratch(MIX_CUTS, ORDERS, HALVES, SHARD, HALF),
+        drain_scratch(QKV_CUTS, QKV_ORDERS, HALVES, SHARD, HALF),
+        drain_scratch(LAST_CUTS, LAST_ORDERS, WHOLE, 16, FLOAT),
+    ]
+    scratch = [pltpu.VMEM((8, 2 * rows, 128), HALF)] * 3
+    scratch += [pltpu.VMEM((8, 2 * mem_rows, 128), HALF), pltpu.VMEM((8, 2 * rows, 256), HALF)]
+    counts = (rows, rows, mem_rows, rows, rows)
+    scratch += [pltpu.VMEM((2, 4, 2, SHARD, size), HALF) for size in counts]
+    scratch += [pltpu.VMEM((4, 2, SHARD, size), HALF) for size in counts]
+    scratch += [
+        pltpu.VMEM((rows, 1024), HALF),
+        pltpu.VMEM((8, rows, 128), HALF),
+        pltpu.VMEM((group, 128), HALF),
+        pltpu.VMEM((group, 256), HALF),
+        pltpu.VMEM((2, 8, 16, 128), FLOAT),
+        pltpu.VMEM((8, 16, 128), FLOAT),
+        pltpu.VMEM((8, 1024), FLOAT),
+    ]
+    for drain in drains:
+        scratch += drain[:-2]
+    scratch.append(pltpu.SemaphoreType.DMA((4,)))
+    for drain in drains:
+        scratch += drain[-2:]
+    scratch += [pltpu.SemaphoreType.DMA((11,))] * 2 + trade_sems() * 4
+    specs = [vmem] * 22
+    for at in (8, 9, 11, 12):
+        specs[at] = anywhere
+    specs[19] = smem
     return pl.pallas_call(
-        scatter_kernel,
-        out_shape=jax.ShapeDtypeStruct((SHARD, WIDTH), FLOAT),
-        in_specs=[pl.BlockSpec(memory_space=pl.ANY)],
-        out_specs=pl.BlockSpec(memory_space=pltpu.VMEM),
+        backward_kernel,
+        out_shape=(
+            shape((rows, 1024), FLOAT),
+            shape((mem_rows, 1024), FLOAT),
+            shape((SHARD, 1152), FLOAT),
+            shape((SHARD, 512), FLOAT),
+            shape((SHARD, 256), FLOAT),
+            shape((16, 128), FLOAT),
+        ),
+        in_specs=specs,
+        out_specs=(vmem, anywhere, vmem, vmem, vmem, vmem),
         scratch_shapes=scratch,
         compiler_params=pltpu.CompilerParams(
-            collective_id=1, has_side_effects=True, vmem_limit_bytes=60 * 2**20
+            collective_id=1, has_side_effects=True, vmem_limit_bytes=64 * 2**20
         ),
-    )(grads.reshape(4, 2, 4, 2, 2, SHARD, WIDTH))
-
-
-def exchange_kernel(src_ref, dst_ref, send_sem, recv_sem, own_sem):
-    me = lax.axis_index("hid")
-    tok = lax.axis_index("tok")
-    barrier = pltpu.get_barrier_semaphore()
-    for step in range(1, 8):
-        pl.semaphore_signal(
-            barrier, inc=1, device_id=(tok, lax.rem(me + step, 8)), device_id_type=MESH
-        )
-    own = pltpu.make_async_copy(src_ref.at[me], dst_ref.at[me], own_sem)
-    own.start()
-    pl.semaphore_wait(barrier, 7)
-    copies = []
-    for step in range(1, 8):
-        target = lax.rem(me + step, 8)
-        copy = pltpu.make_async_remote_copy(
-            src_ref=src_ref.at[target], dst_ref=dst_ref.at[me],
-            send_sem=send_sem.at[step - 1], recv_sem=recv_sem.at[step - 1],
-            device_id=(tok, target), device_id_type=MESH,
-        )
-        copy.start()
-        copies.append(copy)
-    own.wait()
-    for copy in copies:
-        copy.wait()
-
-
-def exchange(blocks, number):
-    return pl.pallas_call(
-        exchange_kernel,
-        out_shape=jax.ShapeDtypeStruct(blocks.shape, blocks.dtype),
-        in_specs=[pl.BlockSpec(memory_space=pl.ANY)],
-        out_specs=pl.BlockSpec(memory_space=pl.ANY),
-        scratch_shapes=[
-            pltpu.SemaphoreType.DMA((7,)),
-            pltpu.SemaphoreType.DMA((7,)),
-            pltpu.SemaphoreType.DMA,
-        ],
-        compiler_params=pltpu.CompilerParams(collective_id=number, has_side_effects=True),
-    )(blocks)
-
-
-def weight_grad_kernel(
-    h1_ref, g1_ref, h2_ref, mem_ref, g2_ref, h3_ref, cot_ref,
-    dqkv_ref, o1_ref, dq2_ref, dkv2_ref, o2_ref, dgu_ref, hid_ref, pad_ref,
-    out_ref,
-):
-    def put(at, left, right):
-        value = dot(left[...], right[0])
-        out_ref[0, :, at : at + value.shape[1]] = value.astype(HALF)
-
-    put(0, h1_ref, dqkv_ref)
-    put(256, g1_ref, o1_ref)
-    put(384, h2_ref, dq2_ref)
-    put(512, mem_ref, dkv2_ref)
-    put(640, g2_ref, o2_ref)
-    put(768, h3_ref, dgu_ref)
-    value = dot(cot_ref[...], hid_ref[0])
-    out_ref[0, :, 1536:1792] = value[:, :256].astype(HALF)
-    out_ref[0, :, 1792:1920] = (value[:, 256:] + pad_ref[0]).astype(HALF)
-
-
-def weight_grads(lefts, rights, pads):
-    return pl.pallas_call(
-        weight_grad_kernel,
-        grid=(8,),
-        out_shape=jax.ShapeDtypeStruct((8, 1024, WIDTH), HALF),
-        in_specs=[pl.BlockSpec(left.shape, lambda j: (0, 0)) for left in lefts]
-        + [
-            pl.BlockSpec((1,) + right.shape[1:], lambda j: (j, 0, 0))
-            for right in rights + [pads]
-        ],
-        out_specs=pl.BlockSpec((1, 1024, WIDTH), lambda j: (j, 0, 0)),
-        compiler_params=pltpu.CompilerParams(vmem_limit_bytes=56 * 2**20),
-    )(*lefts, *rights, pads)
-
-
-def rms_norm(row_vals, gain_vec):
-    return (
-        row_vals * lax.rsqrt(jnp.mean(row_vals * row_vals, axis=-1, keepdims=True) + EPS) * gain_vec
-    )
-
-
-def norm_back(row_vals, gain_vec, gradient):
-    _, pullback = jax.vjp(rms_norm, row_vals, gain_vec)
-    return pullback(gradient)
-
-
-def spread_cols(rows, weights):
-    return jnp.einsum("rd,jdc->jrc", rows, weights, preferred_element_type=FLOAT)
-
-
-def join_cols(blocks, weights):
-    return jnp.einsum("jrc,jdc->rd", blocks, weights, preferred_element_type=FLOAT)
-
-
-def from_windows(sums):
-    sums = sums.reshape(-1, 2, PAIR)
-    tail = jnp.concatenate([sums[1:, :, TILE:], jnp.zeros((1, 2, TILE), FLOAT)], axis=0)
-    return (sums[:, :, :TILE] + tail).transpose(1, 0, 2).reshape(2, -1)
+    )(
+        dq2, dkv2, g2, x1, tokens, memory, h1, h2, o1r, o2r, gains, wa, yff, xt3, xtc, qkv,
+        windows, o1, lse, doc_lens, buckets, dnorm3,
+    )
 
 
 def local(
@@ -1167,80 +1483,38 @@
     ) = forward(packed, small, tokens, memory, doc_lengths, buckets)
     wa = wa.reshape(8, 16 * SHARD, 768)
     wf = wf.reshape(8, 16 * SHARD, 1152)
-    gain_one, gain_two = gains[0], gains[1]
-    onehot = (
-        rel_bucket[:, None] == jnp.arange(32, dtype=jnp.int32)[None, :]
-    ).astype(FLOAT)
-    w_qkv, w_o1, w_q2, w_kv2 = (
-        wa[:, :, 0:256], wa[:, :, 256:384], wa[:, :, 384:512], wa[:, :, 512:640]
-    )
-    rows = tokens.shape[0]
-    group_rows = rows * 8
-    residual = tokens.astype(FLOAT)
     o_two, lse_two = cross_forward(doc_lengths, memory_slot, enc_lengths, q_two, kv_two)
-    o_two_rows, mixed, h_three, hidden, d_gate_up, d_rows, d_out, d_norm3 = middle(
+    o_two_rows, mixed, g_two, d_out, d_norm3, y_ff, xt_three, xt_cot = middle(
         o_two, x_one, cotangent, gains, wa, wf
     )
-    d_norm3 = d_norm3[0]
-    g_two = d_rows.astype(HALF)
     dq_two, dkv_two = cross_backward(
         doc_lengths, memory_slot, enc_lengths, q_two, kv_two, d_out, o_two, lse_two
     )
-    dq_two = exchange(dq_two.reshape(8, rows, 128), 8)
-    dkv_two = exchange(dkv_two.reshape(8, -1, 128), 9)
-    d_memory = join_cols(dkv_two, w_kv2)
-    d_inner, d_norm2 = norm_back(x_one, gain_two, join_cols(dq_two, w_q2))
-    d_rows = d_rows + d_inner
-    g_one = d_rows.astype(HALF)
-    d_out = exchange(spread_cols(g_one, w_o1).astype(HALF), 10).reshape(group_rows, 128)
-    dqkv, diagonals = self_backward(doc_lengths, qkv, windows, d_out, o_one, lse_one)
-    dqkv = exchange(dqkv.reshape(8, rows, 256), 11)
-    d_inner, d_norm1 = norm_back(residual, gain_one, join_cols(dqkv, w_qkv))
-    d_tokens = d_rows + d_inner
-
-    d_table = jnp.dot(onehot.T, from_windows(diagonals).T, precision=HIGH)
-    d_table = jnp.pad(d_table.reshape(16, 2, 2), ((0, 0), (0, SHARD - 2), (0, 0)))
-    d_table = d_table.reshape(1, 16 * SHARD, 2)
-    owned = (jnp.arange(8, dtype=jnp.int32) == hid)[:, None, None]
-    norms = jnp.stack([d_norm1, d_norm2, d_norm3], axis=1)
-    pads = jnp.concatenate(
-        [
-            jnp.broadcast_to(norms[None], (8,) + norms.shape),
-            jnp.where(owned, d_table, 0.0),
-        ],
-        axis=2,
-    )
-    pads = jnp.pad(pads, ((0, 0), (0, 0), (96, 27)))
-    grads = weight_grads(
-        [
-            left.T for left in (h_one, g_one, h_two, memory, g_two, h_three, cotangent)
-        ],
-        [
-            dqkv, o_one_rows, dq_two, dkv_two, o_two_rows,
-            d_gate_up, hidden,
-        ],
-        pads,
-    )
-    shard = scatter_grads(grads)
+    d_tokens, d_memory, ff, mix, qkv_grad, last = backward(
+        dq_two, dkv_two, g_two, x_one, tokens, memory, h_one, h_two, o_one_rows, o_two_rows,
+        gains, wa, y_ff, xt_three, xt_cot, qkv, windows, o_one, lse_one, doc_lengths, buckets,
+        d_norm3,
+    )
+    d_norms = jnp.where(core == 0, last[:3, :SHARD], last[:3, SHARD:])
     return (
         mixed,
         d_tokens,
         d_memory,
-        shard[:, PAD_AT],
-        shard[:, 0:128],
-        shard[:, 128:192],
-        shard[:, 192:256],
-        shard[:, 256:384].T,
-        shard[:2, PAD_AT + 3 : PAD_AT + 5],
-        shard[:, PAD_AT + 1],
-        shard[:, 384:512],
-        shard[:, 512:576],
-        shard[:, 576:640],
-        shard[:, 640:768].T,
-        shard[:, PAD_AT + 2],
-        shard[:, 768:1120],
-        shard[:, 1152:1504],
-        shard[:, 1536:1888].T,
+        d_norms[0],
+        qkv_grad[:, 0:128],
+        qkv_grad[:, 128:192],
+        qkv_grad[:, 192:256],
+        mix[:, 0:128].T,
+        last[3:7, 0].reshape(2, 2),
+        d_norms[1],
+        mix[:, 128:256],
+        mix[:, 256:320],
+        mix[:, 320:384],
+        mix[:, 384:512].T,
+        d_norms[2],
+        ff[:, 0:352],
+        ff[:, 384:736],
+        ff[:, 768:1120].T,
     )
 
 

time: 422 us -> 346 us (0.82)
  Pallas kernels: 347 us -> 312 us
  local copies, waits for them, and re-layouts: 49 us -> 29.7 us
  matrix products: 13.8 us -> 0 us
  other arithmetic: 6.72 us -> 2.28 us
    pallas_call x7 -> x1, Pallas kernels: 168 us -> 131 us  [backward(): pl.pallas_call(backward_kernel, out_shape=(shape((rows, 1024), FLOAT), sh...]
    dot_general x5 -> x0, matrix products: 13.8 us -> none  [the longest x3 10.3 us: join_cols(): jnp.einsum('jrc,jdc->rd', blocks, weights, preferred_element_type=FLOAT)]
    pallas_call x5 -> x0, local copies, waits for them, and re-layouts: 6.69 us -> none  [the longest x3 3.35 us: forward(): pl.pallas_call(forward_kernel, out_shape=(shape(places + (SHARD, 1152), H...]
    pad x2 -> x0, local copies, waits for them, and re-layouts: 5.27 us -> none  [the longest x1 5.27 us: local(): pads = jnp.pad(pads, ((0, 0), (0, 0), (96, 27)))]
    unnamed x84 -> x33, local copies, waits for them, and re-layouts: 16.6 us -> 14 us
where the time goes in v1:
time: 346 us; the launch traced here: 345 us
  Pallas kernels  312 us (90%)
  local copies, waits for them, and re-layouts  29.7 us (9%)
    pallas_call x1, Pallas kernels, backward(): pl.pallas_call(backward_kernel, out_shape=(shape((rows, 1024), FLOAT), sh...  131 us
    pallas_call x1, Pallas kernels, forward(): pl.pallas_call(forward_kernel, out_shape=(shape(places + (SHARD, 1152), H...  116 us
    pallas_call x1, Pallas kernels, middle(): pl.pallas_call(middle_kernel, out_shape=(shape((8, rows, 128), HALF), sha...  32.6 us
    pallas_call x1, Pallas kernels, cross_backward(): pl.pallas_call(cross_backward_kernel, out_shape=(jax.ShapeDtypeStruct((ro...  16.9 us
    pallas_call x1, Pallas kernels, cross_forward(): pl.pallas_call(cross_forward_kernel, out_shape=(jax.ShapeDtypeStruct((row...  15.3 us
    unnamed x33, local copies, waits for them, and re-layouts  14 us

profile of v1, /device:TPU:0, one launch (start us, length us, event | category | flops | bytes accessed | tf_op | source)
XLA Modules:
  0.0 344.9 jit_solution(11403974542823184618)
XLA Ops:
  0.7 0.7 reshape.61
  1.4 0.1 pad.24.clone
  1.5 0.1 pad.25.clone
  1.6 0.7 pad_maximum_fusion
  2.3 0.1 pad_select_fusion
  2.3 0.7 slice.71
  3.0 0.7 maximum_maximum_fusion.small_ref
  3.7 0.7 slice.74
  4.4 0.7 reshape.57
  5.1 0.6 pad.19.bucket_ref
  5.7 0.8 pad.16
  6.5 0.8 pad.17
  7.3 0.8 pad.18
  8.1 1.6 concatenate.18.packed_ref
  9.8 116.1 %shard_map.349 = (bf16[4,2,4,2,2,64,1152]{6,5,4,3,2,1,0:T(8,128)(2,1)}, bf16[4,2,4,2,2,64,768]{6,5,4,3,2,1,0:T(8,128)(2,1)}, f32[8,1024]{1,0:T(8,128)}, f32[16,5...) custom-call(bf16[64,1920]{1,0:T(8,128)(2,1)} %concatenate.18.packed_, ...), custom_call_target="tpu_custom_call" | custom-call | tf_op jit(solution)/shard_map/pallas_call | solution.py:643
  125.9 0.0 copy-start
  125.9 1.1 copy-done
  127.0 1.0 copy-done.4
  128.0 0.7 copy-done.9
  128.7 0.7 copy-done.11
  129.3 0.7 copy-done.13
  130.0 15.3 %shard_map.350 = (bf16[1536,128]{1,0:T(8,128)(2,1)S(1)}, f32[8,512]{1,0:T(8,128)S(1)}) custom-call(s32[1,3]{1,0:T(1,128)S(1)} %copy-done.9, s32[1,3]{1,0:T(1,128)S(1)} %copy-done.11, s32[1,3]{1,0:T(1,128)S(1)} %copy-done.13, bf16[1536,128]{1,0:T(8,128)(2,1)S(1)} %copy-done.4, bf16[3072,128]{1,0:T(8,128)(2,1)S(1)} %copy-done), custom_call_target="tpu_custom_call" | custom-call | tf_op jit(solution)/shard_map/pallas_call | solution.py:160
  145.2 0.0 copy-start.2
  145.2 0.7 copy-done.2
  146.0 0.0 copy-start.12
  146.0 0.0 copy-start.14
  146.0 32.6 %shard_map.351 = (bf16[8,192,128]{2,1,0:T(8,128)(2,1)}, bf16[192,1024]{1,0:T(8,128)(2,1)}, f32[192,1024]{1,0:T(8,128)}, bf16[1536,128]{1,0:T(8,128)(2,1)}, f32[1...) custom-call(bf16[1536,128]{1,0:T(8,128)(2,1)} %copy-done.2, ...), custom_call_target="tpu_custom_call" | custom-call | tf_op jit(solution)/shard_map/pallas_call | solution.py:801
  178.7 0.0 copy-done.1
  178.7 0.0 copy-done.3
  178.7 0.0 copy-done.5
  178.7 0.0 copy-done.10
  178.7 1.0 copy-done.7
  179.7 16.9 %shard_map.352 = (bf16[1536,128]{1,0:T(8,128)(2,1)S(1)}, bf16[3072,128]{1,0:T(8,128)(2,1)S(1)}) custom-call(s32[1,3]{1,0:T(1,128)S(1)} %copy-done.10, s32[1,3]{1,0:T(1,128)S(1)} %copy-done.12, s32[1,3]{1,0:T(1,128)S(1)} %copy-done.14, bf16[1536,128]{1,0:T(8,128)(2,1)S(1)} %copy-done.5, bf16[3072,128]{1,0:T(8,128)(2,1)S(1)} %copy-done.1, ...), custom_call_target="tpu_custom_call" | custom-call | tf_op jit(solution)/shard_map/pallas_call | solution.py:236
  196.6 0.0 copy-start.6
  196.6 0.9 copy-done.6
  197.5 0.7 copy-done.8
  198.2 131.2 %shard_map.353 = (f32[192,1024]{1,0:T(8,128)}, f32[384,1024]{1,0:T(8,128)}, f32[64,1152]{1,0:T(8,128)}, f32[64,512]{1,0:T(8,128)}, f32[64,256]{1,0:T(8,128)}, /*index=5*/f32[16,128]{1,0:T(8,128)}) custom-call(bf16[1536,128]{1,0:T(8,128)(2,1)} %copy-done.8, bf16[3072,128]{1,0:T(8,128)(2,1)} %copy-done.6, f32[192,1024]{1,0:T(8,128)} %get-tuple-element.61.g2_ref, ...), custom_call_target="tpu_custom_call" | custom-call | tf_op jit(solution)/shard_map/pallas_call | solution.py:1431
  329.4 0.8 slice_reduce_fusion
  330.2 0.8 slice_select_fusion
  331.1 0.5 slice_bitcast_fusion.3
  331.6 0.6 reshape_squeeze.3
  332.2 1.4 slice.78
  333.6 1.6 fusion
  335.2 1.4 slice_bitcast_fusion.1
  336.6 1.7 slice_bitcast_fusion
  338.3 1.8 copy.43
  340.1 2.1 copy.44
  342.1 2.7 copy.45
  (14 shorter events, 0.0 us)
Async XLA Ops:
  125.9 1.1 copy-start
  127.0 1.0 copy-start.4
  128.0 0.7 copy-start.9
  128.7 0.7 copy-start.11
  129.3 0.7 copy-start.13
  145.2 0.7 copy-start.2
  146.0 32.7 %copy-start.1 = (bf16[3072,128]{1,0:T(8,128)(2,1)S(1)}, bf16[3072,128]{1,0:T(8,128)(2,1)}, u32[]{:S(2)}) copy-start(bf16[3072,128]{1,0:T(8,128)(2,1)} %get-tuple-element.50.kv_ref) | copy-start | bytes 2359300
  146.0 32.7 %copy-start.3 = (bf16[1536,128]{1,0:T(8,128)(2,1)S(1)}, bf16[1536,128]{1,0:T(8,128)(2,1)}, u32[]{:S(2)}) copy-start(bf16[1536,128]{1,0:T(8,128)(2,1)} %copy-done.2) | copy-start | bytes 1179652
  146.0 32.7 %copy-start.5 = (bf16[1536,128]{1,0:T(8,128)(2,1)S(1)}, bf16[1536,128]{1,0:T(8,128)(2,1)}, u32[]{:S(2)}) copy-start(bf16[1536,128]{1,0:T(8,128)(2,1)} %get-tuple-element.49.q_ref) | copy-start | bytes 1179652
  146.0 32.7 %copy-start.10 = (s32[1,3]{1,0:T(1,128)S(1)}, s32[1,3]{1,0:T(1,128)}, u32[]{:S(2)}) copy-start(s32[1,3]{1,0:T(1,128)} %len_ref.7) | copy-start | bytes 40
  146.0 32.7 %copy-start.12 = (s32[1,3]{1,0:T(1,128)S(1)}, s32[1,3]{1,0:T(1,128)}, u32[]{:S(2)}) copy-start(s32[1,3]{1,0:T(1,128)} %slot_ref.3) | copy-start | bytes 40
  146.0 32.7 %copy-start.14 = (s32[1,3]{1,0:T(1,128)S(1)}, s32[1,3]{1,0:T(1,128)}, u32[]{:S(2)}) copy-start(s32[1,3]{1,0:T(1,128)} %enc_ref.3) | copy-start | bytes 40
  178.7 1.0 copy-start.7
  196.6 0.9 copy-start.6
  197.5 0.7 copy-start.8
